TPU v7x, 32 devices: a whole 2x2x4 slice. The times are simulated.
32 devices in a mesh: seq: 4 (over x, core), ctx: 8 (over z, y).
Axes of the slice: x: 2, y: 2, z: 4, core: 2. Of those that a mesh axis runs over, the one named last changes fastest.
Arguments:
- tokens: bfloat16 [3, 4, 768, 767], P(None, 'seq', 'ctx'), may hold values from -6 to 6
- segment_ids: int32 [3, 4, 768], P(None, 'seq'), may hold values from 0 to 7, never falling along the last dimension, each value on 1 to 576 neighbouring positions
- qkv_weight: bfloat16 [768, 2304], P(('seq', 'ctx')), may hold values from -0.21875 to 0.21875
- out_weight: bfloat16 [768, 767], P(('seq', 'ctx')), may hold values from -0.875 to 0.875
- up_weight: bfloat16 [768, 3072], P(('seq', 'ctx')), may hold values from -0.21875 to 0.21875
- down_weight: bfloat16 [3072, 767], P(('seq', 'ctx')), may hold values from -0.109375 to 0.109375
- attn_gain: bfloat16 [768], P(('seq', 'ctx')), may hold values from 0.099609375 to 1.8984375
- mlp_gain: bfloat16 [768], P(('seq', 'ctx')), may hold values from 0.099609375 to 1.8984375
- out_cotangent: bfloat16 [3, 4, 768, 767], P(None, 'seq', 'ctx'), may hold values from -6 to 6
Outputs:
- result: float32 [3, 4, 768, 767], P(None, 'seq', 'ctx')
- grad_tokens: float32 [3, 4, 768, 767], P(None, 'seq', 'ctx')
- grad_qkv_weight: float32 [768, 2304], P(('seq', 'ctx'))
- grad_out_weight: float32 [768, 767], P(('seq', 'ctx'))
- grad_up_weight: float32 [768, 3072], P(('seq', 'ctx'))
- grad_down_weight: float32 [3072, 767], P(('seq', 'ctx'))
- grad_attn_gain: float32 [768], P(('seq', 'ctx'))
- grad_mlp_gain: float32 [768], P(('seq', 'ctx'))
Inputs may be any that keep to these rules, and one draw needn't show every extreme that they name: `segment_ids`: along each sequence the ids never fall; each of the 8 documents of a sequence has 1 to 576 tokens, and one has exactly 576.
All inputs are finite; a program needn't handle non-finite values.
Results may differ from a plain program's by a relative error of at most 0.014.
Values may be sent and summed in bfloat16 or wider, within the bound.
No kernel may reach another device: no remote copies, remote signals or barrier semaphores. Data moves between devices by JAX's collectives and lax.ppermute only.
A program may use at most 384 MiB of HBM per device.

v0:
```python
import functools
import math

import jax
import jax.numpy as jnp
import numpy as np
from jax import lax
from jax.experimental import pallas as pl
from jax.experimental.pallas import tpu as pltpu
from jax.sharding import PartitionSpec as P

HEADS = 12
HEAD_DIM = 64


EPS = 1e-05
NEG = -1e30
SCALE = 0.125


def crms(inputs, gains):
    totals = jnp.sum(inputs, axis=-1, keepdims=True)
    meansq = (jnp.sum(inputs * inputs, axis=-1, keepdims=True) + totals * totals) / gains.shape[0]
    return jnp.concatenate([inputs, -totals], axis=-1) * lax.rsqrt(meansq + EPS) * gains


def gelu_tanh(inputs):
    return jax.nn.gelu(inputs, approximate=True)


def matmul(left, right):
    return jnp.dot(left, right, preferred_element_type=jnp.float32)


def matmul_left_t(left, right):
    return lax.dot_general(
        left, right, (((0,), (0,)), ((), ())), preferred_element_type=jnp.float32
    )


def matmul_right_t(left, right):
    return lax.dot_general(
        left, right, (((1,), (1,)), ((), ())), preferred_element_type=jnp.float32
    )


def allowed_pairs(query_pos, query_seg, key_pos, key_seg):
    same_doc = query_seg[:, None, :, None] == key_seg[:, None, None, :]
    causal = query_pos[None, None, :, None] >= key_pos[None, None, None, :]
    return same_doc & causal


def attend_block(state, queries, query_pos, query_seg, keys, values, key_pos, key_seg):
    best, denom, accum = state
    scores = (
        jnp.einsum("bqhd,bkhd->bhqk", queries, keys, preferred_element_type=jnp.float32) * SCALE
    )
    allowed = allowed_pairs(query_pos, query_seg, key_pos, key_seg)
    scores = jnp.where(allowed, scores, NEG)
    peak = jnp.maximum(best, jnp.max(scores, axis=-1))
    weights = jnp.where(allowed, jnp.exp(scores - peak[..., None]), 0.0)
    factor = jnp.exp(best - peak)
    denom = denom * factor + jnp.sum(weights, axis=-1)
    accum = accum * factor[..., None] + jnp.einsum(
        "bhqk,bkhd->bhqd", weights.astype(jnp.bfloat16), values, preferred_element_type=jnp.float32
    )
    return (peak, denom, accum)


def pair_grads(queries, grad_o, lse, delta, query_pos, query_seg, keys, values, key_pos, key_seg):
    scores = (
        jnp.einsum("bqhd,bkhd->bhqk", queries, keys, preferred_element_type=jnp.float32) * SCALE
    )
    allowed = allowed_pairs(query_pos, query_seg, key_pos, key_seg)
    probs = jnp.where(allowed, jnp.exp(scores - lse[..., None]), 0.0)
    dprobs = jnp.einsum("bqhd,bkhd->bhqk", grad_o, values, preferred_element_type=jnp.float32)
    grad_scores = (probs * (dprobs - delta[..., None])).astype(jnp.bfloat16)
    part_q = (
        jnp.einsum("bhqk,bkhd->bqhd", grad_scores, keys, preferred_element_type=jnp.float32) * SCALE
    )
    part_k = (
        jnp.einsum("bhqk,bqhd->bkhd", grad_scores, queries, preferred_element_type=jnp.float32)
        * SCALE
    )
    part_v = jnp.einsum(
        "bhqk,bqhd->bkhd", probs.astype(jnp.bfloat16), grad_o, preferred_element_type=jnp.float32
    )
    return (part_q, part_k, part_v)


def body(
    tokens,
    segment_ids,
    qkv_weight,
    out_weight,
    up_weight,
    down_weight,
    attn_gain,
    mlp_gain,
    out_cotangent,
):
    micro_count, seq_count, local_len, res_width = tokens.shape
    length = segment_ids.shape[2]
    first = lax.axis_index("ctx") * local_len
    query_pos = first + jnp.arange(local_len, dtype=jnp.int32)
    row_count = seq_count * local_len

    def fetch():
        return (
            lax.all_gather(qkv_weight, ("seq", "ctx"), axis=0, tiled=True),
            lax.all_gather(out_weight, ("seq", "ctx"), axis=0, tiled=True),
            lax.all_gather(up_weight, ("seq", "ctx"), axis=0, tiled=True),
            lax.all_gather(down_weight, ("seq", "ctx"), axis=0, tiled=True),
            lax.all_gather(attn_gain, ("seq", "ctx"), axis=0, tiled=True),
            lax.all_gather(mlp_gain, ("seq", "ctx"), axis=0, tiled=True),
        )

    def backward(number, gathered, saved):
        qkv_full, out_full, up_full, down_full, gain_one, gain_two = gathered
        (
            inputs,
            seg_rows,
            query_seg,
            norm_a,
            queries,
            keys_own,
            values_own,
            attn_f32,
            lse,
            attn,
            mixed,
            norm_m,
            pre,
            act,
        ) = saved
        width = qkv_full.shape[0]
        grad_y = out_cotangent[number].reshape(row_count, res_width)
        grad_down = matmul_left_t(act, grad_y)
        grad_act = matmul_right_t(grad_y, down_full)
        _, gelu_pull = jax.vjp(gelu_tanh, pre)
        grad_pre = gelu_pull(grad_act)[0].astype(jnp.bfloat16)
        grad_up = matmul_left_t(norm_m, grad_pre)
        grad_norm_m = matmul_right_t(grad_pre, up_full)
        _, pull_two = jax.vjp(crms, mixed, gain_two.astype(jnp.float32))
        grad_mixed_norm, grad_gain_two = pull_two(grad_norm_m)
        grad_mixed = grad_y.astype(jnp.float32) + grad_mixed_norm
        grad_branch = grad_mixed.astype(jnp.bfloat16)
        grad_outw = matmul_left_t(attn, grad_branch)
        grad_attn = (
            matmul_right_t(grad_branch, out_full)
            .astype(jnp.bfloat16)
            .reshape(seq_count, local_len, HEADS, HEAD_DIM)
        )
        delta = jnp.transpose(jnp.sum(grad_attn.astype(jnp.float32) * attn_f32, axis=-1), (0, 2, 1))
        block_len = math.gcd(length, 1024)
        block_ids = jnp.arange(length // block_len, dtype=jnp.int32)
        keys_all, values_all = (
            lax.all_gather(keys_own, "ctx", axis=1, tiled=True),
            lax.all_gather(values_own, "ctx", axis=1, tiled=True),
        )

        def back_keys(carry, number_block):
            offset = number_block * block_len
            key_block = lax.dynamic_slice_in_dim(keys_all, offset, block_len, 1)
            value_block = lax.dynamic_slice_in_dim(values_all, offset, block_len, 1)
            key_pos = offset + jnp.arange(block_len, dtype=jnp.int32)
            key_seg = lax.dynamic_slice_in_dim(seg_rows, offset, block_len, 1)
            part_q, part_k, part_v = pair_grads(
                queries,
                grad_attn,
                lse,
                delta,
                query_pos,
                query_seg,
                key_block,
                value_block,
                key_pos,
                key_seg,
            )
            return (carry + part_q, jnp.concatenate([part_k, part_v], axis=-1))

        grad_q, terms = lax.scan(back_keys, jnp.zeros(queries.shape, jnp.float32), block_ids)
        terms = jnp.moveaxis(terms, 0, 1).reshape(seq_count, length, HEADS, 2 * HEAD_DIM)
        owned_terms = lax.psum_scatter(terms, "ctx", scatter_dimension=1, tiled=True)
        grad_k = owned_terms[..., :HEAD_DIM]
        grad_v = owned_terms[..., HEAD_DIM:]
        grad_qkv = jnp.concatenate(
            [
                grad_q.reshape(row_count, width),
                grad_k.reshape(row_count, width),
                grad_v.reshape(row_count, width),
            ],
            axis=-1,
        ).astype(jnp.bfloat16)
        grad_qkvw = matmul_left_t(norm_a, grad_qkv)
        grad_norm_a = matmul_right_t(grad_qkv, qkv_full)
        _, pull_one = jax.vjp(crms, inputs, gain_one.astype(jnp.float32))
        grad_input_norm, grad_gain_one = pull_one(grad_norm_a)
        grad_inputs = (grad_mixed + grad_input_norm).reshape(seq_count, local_len, res_width)
        return (
            grad_inputs,
            (grad_qkvw, grad_outw, grad_up, grad_down, grad_gain_one, grad_gain_two),
        )

    outputs = []
    input_grads = []
    owned = None
    for number in range(micro_count):
        (
            forward_qkv_full,
            forward_out_full,
            forward_up_full,
            forward_down_full,
            forward_gain_one,
            forward_gain_two,
        ) = fetch()
        forward_width = forward_qkv_full.shape[0]
        forward_inputs = tokens[number].astype(jnp.float32).reshape(row_count, res_width)
        forward_seg_rows = segment_ids[number]
        forward_query_seg = lax.dynamic_slice_in_dim(forward_seg_rows, first, local_len, 1)
        forward_norm_a = crms(forward_inputs, forward_gain_one.astype(jnp.float32)).astype(
            jnp.bfloat16
        )
        qkv = matmul(forward_norm_a, forward_qkv_full).astype(jnp.bfloat16)
        forward_queries = qkv[:, :forward_width].reshape(seq_count, local_len, HEADS, HEAD_DIM)
        forward_keys_own = qkv[:, forward_width : 2 * forward_width].reshape(
            seq_count, local_len, HEADS, HEAD_DIM
        )
        forward_values_own = qkv[:, 2 * forward_width :].reshape(
            seq_count, local_len, HEADS, HEAD_DIM
        )

        def fold_keys(state, piece):
            keys_part, values_part = piece
            span = keys_part.shape[1]
            block_len = span if span <= 1024 else math.gcd(span, 1024)

            def inner(carry, number_block):
                offset = number_block * block_len
                key_block = lax.dynamic_slice_in_dim(keys_part, offset, block_len, 1)
                value_block = lax.dynamic_slice_in_dim(values_part, offset, block_len, 1)
                key_pos = offset + jnp.arange(block_len, dtype=jnp.int32)
                key_seg = lax.dynamic_slice_in_dim(forward_seg_rows, offset, block_len, 1)
                return (
                    attend_block(
                        carry,
                        forward_queries,
                        query_pos,
                        forward_query_seg,
                        key_block,
                        value_block,
                        key_pos,
                        key_seg,
                    ),
                    None,
                )

            state, _ = lax.scan(inner, state, jnp.arange(span // block_len, dtype=jnp.int32))
            return state

        initial = (
            jnp.full((seq_count, HEADS, local_len), NEG, jnp.float32),
            jnp.zeros((seq_count, HEADS, local_len), jnp.float32),
            jnp.zeros((seq_count, HEADS, local_len, HEAD_DIM), jnp.float32),
        )
        best, denom, accum = fold_keys(
            initial,
            (
                lax.all_gather(forward_keys_own, "ctx", axis=1, tiled=True),
                lax.all_gather(forward_values_own, "ctx", axis=1, tiled=True),
            ),
        )
        heads_out = accum / denom[..., None]
        forward_lse = best + jnp.log(denom)
        forward_attn_f32 = jnp.transpose(heads_out, (0, 2, 1, 3))
        forward_attn = forward_attn_f32.reshape(row_count, forward_width).astype(jnp.bfloat16)
        forward_mixed = forward_inputs + matmul(forward_attn, forward_out_full)
        forward_norm_m = crms(forward_mixed, forward_gain_two.astype(jnp.float32)).astype(
            jnp.bfloat16
        )
        forward_pre = matmul(forward_norm_m, forward_up_full)
        forward_act = gelu_tanh(forward_pre).astype(jnp.bfloat16)
        result = (forward_mixed + matmul(forward_act, forward_down_full)).reshape(
            seq_count, local_len, res_width
        )
        forward_saved = (
            forward_inputs,
            forward_seg_rows,
            forward_query_seg,
            forward_norm_a,
            forward_queries,
            forward_keys_own,
            forward_values_own,
            forward_attn_f32,
            forward_lse,
            forward_attn,
            forward_mixed,
            forward_norm_m,
            forward_pre,
            forward_act,
        )
        result, saved = (result, forward_saved)
        grad_inputs, grads = backward(number, fetch(), saved)
        outputs.append(result)
        input_grads.append(grad_inputs)
        shares = (
            lax.psum_scatter(grads[0], ("seq", "ctx"), scatter_dimension=0, tiled=True),
            lax.psum_scatter(grads[1], ("seq", "ctx"), scatter_dimension=0, tiled=True),
            lax.psum_scatter(grads[2], ("seq", "ctx"), scatter_dimension=0, tiled=True),
            lax.psum_scatter(grads[3], ("seq", "ctx"), scatter_dimension=0, tiled=True),
            lax.psum_scatter(grads[4], ("seq", "ctx"), scatter_dimension=0, tiled=True),
            lax.psum_scatter(grads[5], ("seq", "ctx"), scatter_dimension=0, tiled=True),
        )
        owned = shares if owned is None else jax.tree.map(jnp.add, owned, shares)
    return (jnp.stack(outputs), jnp.stack(input_grads)) + tuple(owned)


FLAGS = {'deal': 3, 'cut': 1280, 'shift': 1, 'f0': 0, 'f1': 1, 'f2': 1, 'f3': 1, 'f4': 0, 'f5': 1, 'f6': 1, 'f7': 0, 'f8': 0, 'home': 0, 'b0': 1, 'b1': 0, 'b2': 1, 'b3': 1, 'b4': 0, 'b5': 0, 'b6': 1, 'b7': 0, 'outin': 1, 'dz': 0, 'c': 0, 'dxfirst': 0, 'lz': 0, 'ez': 0, 'dfold': 0, 'ufold': 0, 'upfirst': 1}
SLOTS = 10
LOCAL = 96
WINDOW = 768
ROWS = 3 * LOCAL
KEYS = SLOTS * LOCAL
Z_SWAP = [(i, i ^ 2) for i in range(8)]
Z_FAR = [(i, i ^ 4) for i in range(8)]
Z_SHIFT = [[(i, (i + 2 * k) % 8) for i in range(8)] for k in range(4)]
Y_SWAP = [(i, i ^ 1) for i in range(8)]
X_SWAP = [(i, i ^ 2) for i in range(4)]
CORE_SWAP = [(i, i ^ 1) for i in range(4)]
DEAL = [[(f % 8, f // 3) for f in range(24) if f % 3 == j] for j in range(3)]
RETURN = [[(f // 3, f % 8) for f in range(24) if f % 3 == j] for j in range(3)]
UP = ([(d, d + 1) for d in range(7)], [(0, 2), (2, 4), (3, 5), (5, 7)], [(2, 5)])


def swap_seq(array, pairs):
    return lax.ppermute(array, "seq", pairs)


def swap_ctx(array, pairs):
    return lax.ppermute(array, "ctx", pairs)


def after(value, *others):
    return lax.optimization_barrier((value, others))[0]


def grid_place():
    seq, ctx = lax.axis_index("seq"), lax.axis_index("ctx")
    return seq // 2, seq % 2, ctx // 2, ctx % 2


def along_z(own, *others):
    pair = jnp.stack([own, swap_ctx(own, Z_FAR)])
    return jnp.stack([pair, swap_ctx(after(pair, *others), Z_SWAP)])


def plane_start(line, split):
    left, right = line[..., :split], line[..., split:]
    return jnp.stack([left, swap_seq(left, X_SWAP)]), jnp.stack([right, swap_ctx(right, Y_SWAP)])


def plane_end(left, right):
    return swap_ctx(left, Y_SWAP), swap_seq(right, X_SWAP)


def other_core(pieces):
    return [swap_seq(piece, CORE_SWAP) for piece in pieces]


def place_kernel(cuts, *refs):
    pieces, out_refs, sems = refs[:8], refs[8:-1], refs[-1]
    x, core, z, y = grid_place()
    copies = []
    for i, piece in enumerate(pieces):
        pc = core if i < 4 else 1 - core
        left, far = i % 4 in (0, 2), i % 4 >= 2
        for near in range(2):
            dx, dy = (near, far) if left else (far, near)
            px = 1 - x if dx else x
            py = 1 - y if dy else y
            for low in range(2):
                for high in range(2):
                    pz = z if low == 0 else z + 1 - 2 * (z % 2)
                    pz = pz if high == 0 else (pz + 2) % 4
                    for start, size, out, place in cuts[0 if left else 1]:
                        source = piece.at[near, low, high, :, pl.ds(start, size)]
                        target = out_refs[out].at[px, pc, pz, py]
                        target = target.at[place] if out else target.at[:, pl.ds(place, size)]
                        copies.append((source, target))
    copies = [pltpu.make_async_copy(*ends, sems.at[i]) for i, ends in enumerate(copies)]
    for copy in copies:
        copy.start()
    for copy in copies:
        copy.wait()


def all_rows(own, other, columns, blocks, split, width):
    rows = own[0].shape[-2]
    cuts = ([], [])
    for low, high, side in ((0, split, 0), (split, columns + blocks * width, 1)):
        start, end = low, min(high, columns)
        if end > start:
            cuts[side].append((start - low, end - start, 0, start))
        for block in range(blocks):
            if low <= columns + block * width < high:
                cuts[side].append((columns + block * width - low, width, 1, block))
    shapes = [jax.ShapeDtypeStruct((2, 2, 4, 2, rows, columns), own[0].dtype)]
    if blocks:
        shapes.append(jax.ShapeDtypeStruct((2, 2, 4, 2, blocks, rows, width), own[0].dtype))
    full = pl.pallas_call(
        functools.partial(place_kernel, cuts),
        in_specs=[pl.BlockSpec(memory_space=pltpu.HBM)] * 8,
        out_specs=[pl.BlockSpec(memory_space=pltpu.VMEM)] * len(shapes),
        out_shape=shapes,
        scratch_shapes=[pltpu.SemaphoreType.DMA((32 * (len(cuts[0]) + len(cuts[1])),))],
        compiler_params=pltpu.CompilerParams(vmem_limit_bytes=32 * 1024 * 1024),
        cost_estimate=pl.CostEstimate(
            flops=0, bytes_accessed=128 * rows * (columns + blocks * width), transcendentals=0
        ),
        name="place",
    )(*own, *other)
    return [full[0].reshape(32 * rows, columns)] + [part.reshape(32 * blocks * rows, width) for part in full[1:]]


def pick(array, index, axis):
    return lax.dynamic_index_in_dim(array, index, axis, keepdims=False)


def add_low(left, right):
    return (left.astype(jnp.float32) + right.astype(jnp.float32)).astype(jnp.bfloat16)


def core_rows(left, other):
    _, core, _, _ = grid_place()
    step = left.shape[1] // 4
    first, second, third, fourth = [left[:, i * step : (i + 1) * step] for i in range(4)]
    low = core == (1 if other else 0)
    return jnp.concatenate([jnp.where(low, first, second), jnp.where(low, third, fourth)], axis=1)


def fold_part(part):
    _, core, _, _ = grid_place()
    part = part.reshape(2, 2, 4, 2, -1, part.shape[-1])
    return add_low(pick(part, core, 1), swap_seq(pick(part, 1 - core, 1), CORE_SWAP))


def fold_send(left, right):
    return swap_seq(matmul_left_t(core_rows(left, True), right).astype(jnp.bfloat16), CORE_SWAP)


def fold_core(left, right, got):
    held = (matmul_left_t(core_rows(left, False), right) + got.astype(jnp.float32)).astype(jnp.bfloat16)
    return held.reshape(2, 4, 2, -1, held.shape[-1])


def fold_x(held):
    x, _, _, _ = grid_place()
    return add_low(pick(held, x, 0), swap_seq(pick(held, 1 - x, 0), X_SWAP))


def fold_y(held):
    _, _, _, y = grid_place()
    axis = held.ndim - 3
    return add_low(pick(held, y, axis), swap_ctx(pick(held, 1 - y, axis), Y_SWAP))


def fold_start(left, right):
    return fold_x(left), fold_y(right)


def fold_end(left, right):
    return jnp.concatenate([fold_y(left), fold_x(right)], axis=-1)


def halves(held):
    half = held.shape[-1] // 2
    return held[..., :half], held[..., half:]


def fold_z(line):
    _, _, z, _ = grid_place()
    total = pick(line, z, 0).astype(jnp.float32)
    for k in range(1, 4):
        total = total + swap_ctx(pick(line, (z + k) % 4, 0), Z_SHIFT[k]).astype(jnp.float32)
    return total


def fold_near_z(line):
    _, _, z, _ = grid_place()
    pairs = line.reshape((2, 2) + line.shape[1:])
    return add_low(pick(pairs, z % 2, 1), swap_ctx(pick(pairs, 1 - z % 2, 1), Z_SWAP))


def fold_far_z(held):
    _, _, z, _ = grid_place()
    got = swap_ctx(pick(held, 1 - z // 2, 0), Z_FAR)
    return pick(held, z // 2, 0).astype(jnp.float32) + got.astype(jnp.float32)


def norm_parts(rows):
    width = rows.shape[-1]
    totals = jnp.sum(rows, axis=-1, keepdims=True)
    meansq = (jnp.sum(rows * rows, axis=-1, keepdims=True) + totals * totals) / width
    scale = lax.rsqrt(meansq + EPS)
    last = lax.broadcasted_iota(jnp.int32, rows.shape, 1) == width - 1
    return jnp.where(last, -totals, rows) * scale, scale


def norm_back(normed, scale, gains, grads):
    width = normed.shape[-1]
    weighted = grads * gains
    mean = jnp.sum(weighted * normed, axis=-1, keepdims=True) / width
    grad_u = scale * (weighted - normed * mean)
    last = lax.broadcasted_iota(jnp.int32, grad_u.shape, 1) == width - 1
    final = jnp.sum(jnp.where(last, grad_u, 0.0), axis=-1, keepdims=True)
    return jnp.where(last, 0.0, grad_u - final)


def stack_heads(block):
    head = lax.broadcasted_iota(jnp.int32, block.shape, 1) // HEAD_DIM
    return jnp.concatenate([jnp.where(head == i, block, jnp.zeros_like(block)) for i in range(4)], axis=0)


def unstack_heads(turned):
    rows = turned.T
    head = lax.broadcasted_iota(jnp.int32, (LOCAL, 4 * HEAD_DIM), 1) // HEAD_DIM
    picked = rows[:LOCAL]
    for i in range(1, 4):
        picked = jnp.where(head == i, rows[i * LOCAL : (i + 1) * LOCAL], picked)
    return picked


def attend_kernel(starts, q_ref, k_ref, v_ref, key_ref, query_ref, out_ref, probs_ref, bias_ref):
    window = pl.ds(pl.multiple_of(starts[pl.program_id(0)], 32), WINDOW)

    @pl.when(pl.program_id(1) == 0)
    def _():
        same = key_ref[window, 0:1] == query_ref[0, 0:1, :]
        causal = key_ref[window, 1:2] <= query_ref[0, 1:2, :]
        bias_ref[...] = jnp.where(same & causal, 0.0, NEG)

    stacked = stack_heads(q_ref[...])
    scores = matmul_right_t(k_ref[window, :], stacked) + bias_ref[...]
    weights = jnp.exp(scores - jnp.max(scores, axis=0, keepdims=True))
    probs = (weights * (1.0 / jnp.sum(weights, axis=0, keepdims=True))).astype(jnp.bfloat16)
    probs_ref[0, 0] = probs
    out_ref[...] = unstack_heads(matmul(v_ref[window, :].T, probs)).astype(jnp.bfloat16)


def attend(queries, keys, values, starts, key_marks, query_marks):
    return pl.pallas_call(
        attend_kernel,
        grid_spec=pltpu.PrefetchScalarGridSpec(
            num_scalar_prefetch=1,
            grid=(3, 3),
            in_specs=[
                pl.BlockSpec((LOCAL, 256), lambda j, h, s: (j, h)),
                pl.BlockSpec((KEYS, 256), lambda j, h, s: (0, h)),
                pl.BlockSpec((KEYS, 256), lambda j, h, s: (0, h)),
                pl.BlockSpec((KEYS, 2), lambda j, h, s: (0, 0)),
                pl.BlockSpec((1, 2, 4 * LOCAL), lambda j, h, s: (j, 0, 0)),
            ],
            out_specs=[
                pl.BlockSpec((LOCAL, 256), lambda j, h, s: (j, h)),
                pl.BlockSpec((1, 1, WINDOW, 4 * LOCAL), lambda j, h, s: (j, h, 0, 0)),
            ],
            scratch_shapes=[pltpu.VMEM((WINDOW, 4 * LOCAL), jnp.float32)],
        ),
        out_shape=[
            jax.ShapeDtypeStruct((ROWS, 768), jnp.bfloat16),
            jax.ShapeDtypeStruct((3, 3, WINDOW, 4 * LOCAL), jnp.bfloat16),
        ],
        compiler_params=pltpu.CompilerParams(vmem_limit_bytes=40 * 1024 * 1024),
        cost_estimate=pl.CostEstimate(flops=3_000_000_000, bytes_accessed=12_000_000, transcendentals=2_700_000),
        name="attend",
    )(starts, queries, keys, values, key_marks, query_marks)


def attend_back_kernel(
    starts, q_ref, k_ref, v_ref, grad_ref, probs_ref, grad_q_ref, grad_k_ref, grad_v_ref, sum_k, sum_v
):
    row_block = pl.program_id(1)
    window = pl.ds(pl.multiple_of(starts[row_block], 32), WINDOW)

    @pl.when(row_block == 0)
    def _():
        sum_k[...] = jnp.zeros_like(sum_k)
        sum_v[...] = jnp.zeros_like(sum_v)

    probs = probs_ref[0, 0]
    grads = stack_heads(grad_ref[...])
    wide = probs.astype(jnp.float32)
    terms = wide * matmul_right_t(v_ref[window, :], grads)
    grad_scores = (terms - wide * jnp.sum(terms, axis=0, keepdims=True)).astype(jnp.bfloat16)
    sum_v[window, :] += matmul(probs, grads)
    sum_k[window, :] += matmul(grad_scores, stack_heads(q_ref[...]))
    grad_q = unstack_heads(matmul(k_ref[window, :].T, grad_scores)) * SCALE
    grad_q_ref[...] = grad_q.astype(jnp.bfloat16)

    @pl.when(row_block == 2)
    def _():
        grad_k_ref[...] = sum_k[...].astype(jnp.bfloat16)
        grad_v_ref[...] = sum_v[...].astype(jnp.bfloat16)


def attend_back(queries, keys, values, grads, probs, starts):
    return pl.pallas_call(
        attend_back_kernel,
        grid_spec=pltpu.PrefetchScalarGridSpec(
            num_scalar_prefetch=1,
            grid=(3, 3),
            in_specs=[
                pl.BlockSpec((LOCAL, 256), lambda h, j, s: (j, h)),
                pl.BlockSpec((KEYS, 256), lambda h, j, s: (0, h)),
                pl.BlockSpec((KEYS, 256), lambda h, j, s: (0, h)),
                pl.BlockSpec((LOCAL, 256), lambda h, j, s: (j, h)),
                pl.BlockSpec((1, 1, WINDOW, 4 * LOCAL), lambda h, j, s: (j, h, 0, 0)),
            ],
            out_specs=[
                pl.BlockSpec((LOCAL, 256), lambda h, j, s: (j, h)),
                pl.BlockSpec((KEYS, 256), lambda h, j, s: (0, h)),
                pl.BlockSpec((KEYS, 256), lambda h, j, s: (0, h)),
            ],
            scratch_shapes=[pltpu.VMEM((KEYS, 256), jnp.float32), pltpu.VMEM((KEYS, 256), jnp.float32)],
        ),
        out_shape=[
            jax.ShapeDtypeStruct((ROWS, 768), jnp.bfloat16),
            jax.ShapeDtypeStruct((KEYS, 768), jnp.bfloat16),
            jax.ShapeDtypeStruct((KEYS, 768), jnp.bfloat16),
        ],
        compiler_params=pltpu.CompilerParams(vmem_limit_bytes=40 * 1024 * 1024),
        cost_estimate=pl.CostEstimate(flops=7_000_000_000, bytes_accessed=14_000_000, transcendentals=0),
        name="attend_back",
    )(starts, queries, keys, values, grads, probs)


def widen(array):
    return jnp.pad(array, [(0, 0)] * (array.ndim - 1) + [(0, 1)])


def send_home(delta):
    delta = delta.reshape(3, -1, delta.shape[-1])
    return [swap_ctx(delta[j], RETURN[j]) for j in range(3)]


def at_home(parts, base, ctx):
    home = jnp.zeros((3,) + parts[0].shape, parts[0].dtype)
    for j, part in enumerate(parts):
        home = lax.dynamic_update_index_in_dim(home, part, (2 * j + ctx) % 3, 0)
    return base.astype(jnp.float32) + home[..., : base.shape[-1]].astype(jnp.float32)


def spread_body(
    tokens,
    segment_ids,
    qkv_weight,
    out_weight,
    up_weight,
    down_weight,
    attn_gain,
    mlp_gain,
    out_cotangent,
):
    micro_count, _, local_len, res_width = tokens.shape
    width = res_width + 1
    ctx = lax.axis_index("ctx")
    tokens = tokens.reshape(micro_count, local_len, res_width)
    cotangent = out_cotangent.reshape(micro_count, local_len, res_width)

    gains_own = jnp.pad(jnp.stack([attn_gain, mlp_gain], axis=1), ((0, 0), (0, 126)))
    rows_own, ff = up_weight.shape
    def deal(array):
        return [swap_ctx(pick(array, (2 * j + ctx) % 3, 0), DEAL[j]) for j in range(3)]

    def meet(flag, *values):
        return lax.optimization_barrier(values) if FLAGS[flag] else values

    wide, cotangent_wide = widen(tokens), widen(cotangent)
    if FLAGS["deal"] == 1:
        both = deal(jnp.concatenate([wide, cotangent_wide], axis=1))
        dealt = [part[:local_len] for part in both]
        grad_rows = [part[local_len:] for part in both]
    else:
        dealt, grad_rows = deal(wide), []
    far = swap_ctx(wide[1], [(0, 5)])
    early_own = jnp.concatenate([qkv_weight, gains_own], axis=1)
    early_cut = FLAGS["cut"]
    up_own, down_own = jnp.concatenate([widen(out_weight), up_weight], axis=1), widen(down_weight)
    pair = jnp.stack([early_own, swap_ctx(early_own, Z_FAR)])
    pair, up_own, down_own = meet("f0", pair, up_own, down_own)
    line = jnp.stack([pair, swap_ctx(pair, Z_SWAP)])
    dealt, far, line, up_own, down_own, cotangent_wide, grad_rows = meet(
        "f1", dealt, far, line, up_own, down_own, cotangent_wide, grad_rows
    )
    inputs_low = jnp.concatenate(dealt, axis=0)
    near = plane_start(line, early_cut)
    up_own = after(up_own, line)
    up_pair = jnp.stack([up_own, swap_ctx(up_own, Z_FAR)])
    if FLAGS["deal"] == 0:
        grad_rows = [swap_ctx(pick(cotangent_wide, (2 * j + ctx) % 3, 0), DEAL[j]) for j in range(2)]
    near, up_pair, inputs_low = meet("f2", near, up_pair, inputs_low)
    ends = plane_end(*near)
    up_line = jnp.stack([up_pair, swap_ctx(up_pair, Z_SWAP)])
    if FLAGS["deal"] == 0:
        grad_rows.append(swap_ctx(pick(cotangent_wide, (4 + ctx) % 3, 0), DEAL[2]))
    up_line, ends, inputs_low, grad_rows = meet("f3", up_line, ends, inputs_low, grad_rows)
    pieces = [*near, *ends]
    others = other_core(pieces)
    up_near = plane_start(up_line, (width + ff) // 2)
    down_own = after(down_own, up_line)
    down_pair = jnp.stack([down_own, swap_ctx(down_own, Z_FAR)])
    below = [None, None]
    if FLAGS["shift"] in (0, 1):
        below[0] = swap_ctx(inputs_low, UP[0])
    if FLAGS["shift"] == 0:
        below[1] = swap_ctx(inputs_low, UP[1])
    up_near, down_pair, others, below, inputs_low, cotangent_wide = meet(
        "f4", up_near, down_pair, others, below, inputs_low, cotangent_wide
    )
    (first,) = all_rows(pieces, others, early_own.shape[1], 0, early_cut, width)
    up_ends = plane_end(*up_near)
    down_line = jnp.stack([down_pair, swap_ctx(down_pair, Z_SWAP)])
    if FLAGS["shift"] == 2:
        below[0] = swap_ctx(inputs_low, UP[0])
    if FLAGS["shift"] in (1, 2):
        below[1] = swap_ctx(inputs_low, UP[1])
    down_line, up_ends, below, _ = meet("f5", down_line, up_ends, below, first)
    if FLAGS["deal"] == 3:
        grad_rows = deal(cotangent_wide)
    down_near = plane_start(down_line, width // 2)
    up_others = other_core([*up_near, *up_ends])
    key_rows = jnp.concatenate([far, below[1], below[0], inputs_low], axis=0).astype(jnp.float32)
    q_full, second = first[:, :width], first[:, width : 3 * width]
    gain_one = first[:, 3 * width].astype(jnp.float32)
    gain_two = first[:, 3 * width + 1].astype(jnp.float32)

    ids = segment_ids.reshape(micro_count, -1) + 8 * jnp.arange(micro_count, dtype=jnp.int32)[:, None]
    ids = jnp.concatenate([jnp.full((KEYS - ROWS,), -1, jnp.int32), ids.reshape(-1)])
    ids = lax.dynamic_slice_in_dim(ids, ROWS * ctx, KEYS, 0)
    places = jnp.arange(KEYS, dtype=jnp.int32)
    key_marks = jnp.stack([ids, places], axis=1)
    query_marks = jnp.stack([ids, places])[:, KEYS - ROWS :].reshape(2, 3, local_len)
    query_marks = jnp.tile(jnp.moveaxis(query_marks, 0, 1), (1, 1, 4))
    flat = 3 * ctx + jnp.arange(3, dtype=jnp.int32)
    starts = jnp.clip(8 * (flat // 8) + 7 - 3 * ctx, 0, 2) * local_len

    inputs = key_rows[KEYS - ROWS :]
    key_normed, key_scale = norm_parts(key_rows)
    norm_keys = (key_normed * gain_one).astype(jnp.bfloat16)
    norm_a = norm_keys[KEYS - ROWS :]
    queries = (matmul(norm_a, q_full).astype(jnp.bfloat16) * SCALE).astype(jnp.bfloat16)
    keys_values = matmul(norm_keys, second).astype(jnp.bfloat16)
    keys, values = keys_values[:, :width], keys_values[:, width:]
    queries, keys, values, down_near, up_others = meet("f6", queries, keys, values, down_near, up_others)
    down_ends = plane_end(*down_near)
    if FLAGS["deal"] == 2:
        grad_rows = deal(cotangent_wide)
    attn, probs = attend(queries, keys, values, starts, key_marks, query_marks)
    attn, down_ends, up_others, grad_rows = meet("f7", attn, down_ends, up_others, grad_rows)
    grad_rows = jnp.concatenate(grad_rows, axis=0)
    down_pieces = [*down_near, *down_ends]
    down_others = other_core(down_pieces)
    (out_up_full,) = all_rows([*up_near, *up_ends], up_others, width + ff, 0, (width + ff) // 2, width)
    out_full, up_full = out_up_full[:, :width], out_up_full[:, width:]
    branch = matmul(attn, out_full)
    mixed = inputs + branch
    mixed_normed, mixed_scale = norm_parts(mixed)
    norm_m, down_others = meet("f8", (mixed_normed * gain_two).astype(jnp.bfloat16), down_others)
    (down_full,) = all_rows(down_pieces, down_others, width, 0, width // 2, width)
    pre = matmul(norm_m, up_full)
    act, gelu_pull = jax.vjp(gelu_tanh, pre)
    act = act.astype(jnp.bfloat16)

    if FLAGS["dfold"]:
        down_got = fold_send(act, grad_rows)
    else:
        grad_down = matmul_left_t(act, grad_rows).astype(jnp.bfloat16)
        grad_rows = after(grad_rows, grad_down)
        down_got = fold_part(grad_down)
    grad_pre = gelu_pull(matmul_right_t(grad_rows, down_full))[0].astype(jnp.bfloat16)
    result_delta = (branch + matmul(act, down_full)).astype(jnp.bfloat16)
    deltas = result_delta.reshape(3, local_len, width)
    home = []
    if FLAGS["home"] == 1:
        home = send_home(result_delta)
    down_got, grad_pre = meet("b0", down_got, grad_pre)
    down_near = fold_start(*halves(fold_core(act, grad_rows, down_got) if FLAGS["dfold"] else down_got))
    if FLAGS["ufold"]:
        up_got = fold_send(norm_m, grad_pre)
    else:
        grad_up = matmul_left_t(norm_m, grad_pre).astype(jnp.bfloat16)
        up_held = fold_part(grad_up)
        if FLAGS["upfirst"]:
            grad_pre = after(grad_pre, grad_up)
    grad_norm_m = matmul_right_t(grad_pre, up_full)
    grad_gain_two = jnp.sum(grad_norm_m * mixed_normed, axis=0)
    grad_mixed_norm = norm_back(mixed_normed, mixed_scale, gain_two, grad_norm_m)
    grad_branch = (grad_rows.astype(jnp.float32) + grad_mixed_norm).astype(jnp.bfloat16)
    grad_attn = matmul_right_t(grad_branch, out_full).astype(jnp.bfloat16)
    if FLAGS["ufold"]:
        up_held = fold_core(norm_m, grad_pre, up_got)
    if FLAGS["outin"]:
        grad_out = matmul_left_t(attn, grad_branch).astype(jnp.bfloat16)
        grad_attn, grad_out = meet("b1", grad_attn, grad_out)
    grad_attn, grad_branch, down_near, up_held, home, deltas = meet(
        "b2", grad_attn, grad_branch, down_near, up_held, home, deltas
    )
    down_line, up_near = fold_end(*down_near), fold_start(*halves(up_held))
    if FLAGS["home"] == 2:
        home = [swap_ctx(deltas[0], RETURN[0])]
    grad_q, grad_k, grad_v = attend_back(queries, keys, values, grad_attn, probs, starts)
    grad_q, grad_k, grad_v, down_line, up_near, home, deltas = meet(
        "b3", grad_q, grad_k, grad_v, down_line, up_near, home, deltas
    )
    if FLAGS["home"] == 2:
        home = home + [swap_ctx(deltas[j], RETURN[j]) for j in (1, 2)]
    up_line = fold_end(*up_near)
    if FLAGS["dz"]:
        down_pair = fold_near_z(down_line)
    grad_kv = jnp.concatenate([grad_k, grad_v], axis=1)
    grad_norm_keys = matmul_right_t(grad_kv, second)
    grad_below = grad_norm_keys[: KEYS - ROWS].astype(jnp.bfloat16)
    sent = [grad_below[4 * local_len :], grad_below[local_len : 4 * local_len], grad_below[:local_len]]
    back = []
    for part, pairs in zip(sent, UP):
        if FLAGS["c"] and len(back) == 2:
            part = after(part, back)
        back.append(swap_ctx(part, [(high, low) for low, high in pairs]))
    if FLAGS["dxfirst"]:
        grad_kv, grad_q = after((grad_kv, grad_q), grad_below)
    grad_norm_q = matmul_right_t(grad_q, q_full)
    grad_gain_one = jnp.sum(grad_norm_keys * key_normed, axis=0)
    grad_gain_one = grad_gain_one + jnp.sum(grad_norm_q * key_normed[KEYS - ROWS :], axis=0)
    gains = jnp.pad(jnp.stack([grad_gain_one, grad_gain_two], axis=1).astype(jnp.bfloat16), ((0, 0), (0, 126)))
    _, core, _, _ = grid_place()
    grad_q_weight = matmul_left_t(norm_a, grad_q).astype(jnp.bfloat16)
    grad_kv_weight = matmul_left_t(norm_keys, grad_kv).astype(jnp.bfloat16)
    if not FLAGS["outin"]:
        grad_out = matmul_left_t(attn, grad_branch).astype(jnp.bfloat16)
    early_parts = [part.reshape(2, 2, 8 * rows_own, -1) for part in (grad_q_weight, grad_kv_weight, grad_out, gains)]
    early_got = swap_seq(jnp.concatenate([pick(part, 1 - core, 1) for part in early_parts], axis=-1), CORE_SWAP)
    early_held = add_low(jnp.concatenate([pick(part, core, 1) for part in early_parts], axis=-1), early_got)
    early_held, up_line = meet("b4", early_held, up_line)
    if FLAGS["home"] != 0:
        home, up_line = meet("b5", home, up_line)
        result = at_home(home, tokens, ctx)
    early_held = early_held.reshape(2, 4, 2, rows_own, -1)
    early_left, early_right = early_held[..., : 2 * width], early_held[..., 2 * width :]
    early_near = fold_start(early_left, early_right)
    if not FLAGS["dz"]:
        up_line = jnp.concatenate(
            [up_line] + [down_line[:, i * rows_own : (i + 1) * rows_own] for i in range(4)], axis=2
        )
    if FLAGS["lz"] == 0:
        up_pair = fold_near_z(up_line)
        early_near, back, up_pair = meet("b6", early_near, back, up_pair)
    else:
        early_near, back, up_line = meet("b6", early_near, back, up_line)
        up_pair = fold_near_z(up_line)
    early_line = fold_end(*early_near)
    early_line, up_pair = meet("b7", early_line, up_pair)
    grad_norm_a = grad_norm_keys[KEYS - ROWS :] + grad_norm_q + back[0].astype(jnp.float32) + back[1].astype(jnp.float32)
    grad_norm_a = grad_norm_a + jnp.pad(back[2].astype(jnp.float32), ((2 * local_len, 0), (0, 0)))
    grad_input_norm = norm_back(
        key_normed[KEYS - ROWS :], key_scale[KEYS - ROWS :], gain_one, grad_norm_a
    )
    grad_delta = (grad_mixed_norm + grad_input_norm).astype(jnp.bfloat16)
    if FLAGS["ez"]:
        early_sum = fold_far_z(fold_near_z(early_line))
    else:
        early_sum = fold_z(early_line)
    if FLAGS["home"] == 0:
        deltas = jnp.stack([deltas, grad_delta.reshape(3, local_len, width)], axis=1)
        parts = send_home(deltas)
        result = at_home([part[:local_len] for part in parts], tokens, ctx)
        grad_tokens = at_home([part[local_len:] for part in parts], cotangent, ctx)
    else:
        grad_tokens = at_home(send_home(grad_delta), cotangent, ctx)
    late_sum = fold_far_z(up_pair)
    grad_up = late_sum[:, :ff]
    if FLAGS["dz"]:
        grad_down = fold_far_z(down_pair)
    else:
        grad_down = jnp.concatenate([late_sum[:, ff + i * width : ff + (i + 1) * width] for i in range(4)], axis=0)
    grad_qkv, grad_out = early_sum[:, : 3 * width], early_sum[:, 3 * width : 4 * width]
    grad_gain_one, grad_gain_two = early_sum[:, 4 * width], early_sum[:, 4 * width + 1]
    shape = (micro_count, 1, local_len, res_width)
    return (
        result.reshape(shape),
        grad_tokens.reshape(shape),
        grad_qkv,
        grad_out[:, :res_width],
        grad_up,
        grad_down[:, :res_width],
        grad_gain_one,
        grad_gain_two,
    )


def solution(mesh):
    small = (mesh.shape["seq"], mesh.shape["ctx"]) == (4, 8)
    return jax.shard_map(
        spread_body if small else body,
        mesh=mesh,
        in_specs=(
            P(None, "seq", "ctx", None),
            P(None, "seq", None),
            P(("seq", "ctx"), None),
            P(("seq", "ctx"), None),
            P(("seq", "ctx"), None),
            P(("seq", "ctx"), None),
            P(("seq", "ctx")),
            P(("seq", "ctx")),
            P(None, "seq", "ctx", None),
        ),
        out_specs=(
            P(None, "seq", "ctx", None),
            P(None, "seq", "ctx", None),
            P(("seq", "ctx"), None),
            P(("seq", "ctx"), None),
            P(("seq", "ctx"), None),
            P(("seq", "ctx"), None),
            P(("seq", "ctx")),
            P(("seq", "ctx")),
        ),
        check_vma=False,
    )
```

profile of v0, /device:TPU:0, one launch (start us, length us, event | category | flops | bytes accessed | tf_op | source)
XLA Modules:
  0.0 322.8 jit_solution(3655313644891944438)
XLA Ops:
  2.4 4.1 %collective-permute-start.4 = (bf16[24,2432]{1,0:T(8,128)(2,1)S(1)}, bf16[24,2432]{1,0:T(8,128)(2,1)S(1)}, u32[]{:S(2)}, u32[]{:S(2)}) collective-permute-start(bf16[24,2432]{1,0:T(8,128)(2,1)S(1)} %get-tuple-element.228), channel_id=1, source_target_pairs={{0,4},{1,5},{2,6},{3,7},{4,0},{5,1},{6,2},{7,3},{8,12},{9,13},{10,... | collective-permute-start | bytes 350216 | tf_op jit(solution)/shard_map/ppermute | solution.py:340
  7.7 3.2 collective-permute-start.3
  10.9 1.9 collective-permute-start.2
  13.5 2.6 collective-permute-start.1
  19.8 7.0 %collective-permute-done.5 = bf16[2,24,2432]{2,1,0:T(8,128)(2,1)S(1)} collective-permute-done((bf16[2,24,2432]{2,1,0:T(8,128)(2,1)S(1)}, bf16[2,24,2432]{2,1,0:T(8,128)(2,1)S(1)}, u32[]{:S(2)}, u32[]{:S(2)}) %collective-permute-start.5) | collective-permute-done | bytes 233504 | tf_op jit(solution)/shard_map/ppermute | solution.py:340
  28.0 2.2 collective-permute-start.7
  32.5 4.4 %collective-permute-done.8 = bf16[24,3840]{1,0:T(8,128)(2,1)S(1)} collective-permute-done((bf16[24,3840]{1,0:T(8,128)(2,1)S(1)}, bf16[24,3840]{1,0:T(8,128)(2,1)S(1)}, u32[]{:S(2)}, u32[]{:S(2)}) %collective-permute-start.8) | collective-permute-done | bytes 184352 | tf_op jit(solution)/shard_map/ppermute | solution.py:340
  37.1 2.1 collective-permute-start.9
  40.6 2.8 collective-permute-start.30
  44.9 2.1 collective-permute-done.9
  47.1 7.4 %collective-permute-done.11.refs_3_ = bf16[2,2,2,24,1152]{4,3,2,1,0:T(8,128)(2,1)} collective-permute-done((bf16[2,2,2,24,1152]{4,3,2,1,0:T(8,128)(2,1)S(1)}, bf16[2,2,2,24,1152]{4,3,2,1,0:T(8,128)(2,1)}, u32[]{:S(2)}, u32[]{:S(2)}) %collective-permute-start.11) | collective-permute-done | bytes 442400 | tf_op jit(solution)/shard_map/ppermute | solution.py:336
  56.3 2.9 collective-permute-start.12
  60.5 3.1 collective-permute-start.32
  63.6 3.2 %collective-permute-start.31 = (bf16[96,768]{1,0:T(8,128)(2,1)}, bf16[96,768]{1,0:T(8,128)(2,1)S(1)}, u32[]{:S(2)}, u32[]{:S(2)}) collective-permute-start(bf16[96,768]{1,0:T(8,128)(2,1)} %get-tuple-element.211), channel_id=1, source_target_pairs={{1,0},{4,1},{7,2},{2,3},{5,4},{0,5},{3,6},{6,7},{9,8},{12,9},{15,1... | collective-permute-start | bytes 442376 | tf_op jit(solution)/shard_map/ppermute | solution.py:340
  71.2 3.5 %collective-permute-done.14 = bf16[2,2,24,1920]{3,2,1,0:T(8,128)(2,1)S(1)} collective-permute-done((bf16[2,2,24,1920]{3,2,1,0:T(8,128)(2,1)S(1)}, bf16[2,2,24,1920]{3,2,1,0:T(8,128)(2,1)S(1)}, u32[]{:S(2)}, u32[]{:S(2)}) %collective-permute-start.14) | collective-permute-done | bytes 368672 | tf_op jit(solution)/shard_map/ppermute | solution.py:336
  74.9 3.9 %collective-permute-done.13 = bf16[2,96,768]{2,1,0:T(8,128)(2,1)S(1)} collective-permute-done((bf16[2,96,768]{2,1,0:T(8,128)(2,1)S(1)}, bf16[2,96,768]{2,1,0:T(8,128)(2,1)S(1)}, u32[]{:S(2)}, u32[]{:S(2)}) %collective-permute-start.13) | collective-permute-done | bytes 294944 | tf_op jit(solution)/shard_map/ppermute | solution.py:340
  80.4 3.3 %collective-permute-start.19 = (bf16[288,768]{1,0:T(8,128)(2,1)}, bf16[288,768]{1,0:T(8,128)(2,1)}, u32[]{:S(2)}, u32[]{:S(2)}) collective-permute-start(bf16[288,768]{1,0:T(8,128)(2,1)} %pad_maximum_fusion.12), channel_id=1, source_target_pairs={{0,2},{2,4},{3,5},{5,7},{8,10},{10,12},{11,13},{13,15},{16,18},{18... | collective-permute-start | bytes 1327112 | tf_op jit(solution)/shard_map/ppermute | solution.py:340
  83.6 2.4 collective-permute-start.18
  86.2 2.2 place.3
  88.4 1.8 copy-done.1
  90.7 1.6 collective-permute-done.19
  92.3 8.9 %collective-permute-done.18 = bf16[288,768]{1,0:T(8,128)(2,1)} collective-permute-done((bf16[288,768]{1,0:T(8,128)(2,1)}, bf16[288,768]{1,0:T(8,128)(2,1)}, u32[]{:S(2)}, u32[]{:S(2)}) %collective-permute-start.18) | collective-permute-done | bytes 442400 | tf_op jit(solution)/shard_map/ppermute | solution.py:340
  102.4 2.5 collective-permute-start.25
  105.4 1.8 convert_reduce_fusion
  107.3 1.8 multiply_convert_fusion.1
  109.1 2.4 convolution_convert_fusion.2
  112.3 1.6 collective-permute-start.24
  115.5 5.8 %collective-permute-done.24 = bf16[2,2,96,384]{3,2,1,0:T(8,128)(2,1)S(1)} collective-permute-done((bf16[2,2,96,384]{3,2,1,0:T(8,128)(2,1)S(1)}, bf16[2,2,96,384]{3,2,1,0:T(8,128)(2,1)S(1)}, u32[]{:S(2)}, u32[]{:S(2)}) %collective-permute-start.24) | collective-permute-done | bytes 294944 | tf_op jit(solution)/shard_map/ppermute | solution.py:336
  123.4 2.9 place.4
  126.4 13.1 %attend.1 = (bf16[288,768]{1,0:T(8,128)(2,1)S(1)}, bf16[3,3,768,384]{3,2,1,0:T(8,128)(2,1)S(1)}) custom-call(s32[3]{0:T(128)S(1)} %clamp_multiply_fusion.starts, bf16[288,768]{1,0:T(8,128)(2,1)S(1)} %fusion.18.q_ref, bf16[960,768]{1,0:T(8,128)(2,1)S(1)} %get-tuple-element.90.k_ref, bf16[960,768]{1,0:T(8,128)(2,1)S(1)} %get-tuple-element.91.v_ref, ...), custom_call_target="tpu_custom_call" | custom-call | flops 3000000000 | bytes 12000000 | tf_op jit(solution)/shard_map/attend/pallas_call | solution.py:551
  139.5 1.9 fusion.75
  141.5 1.6 fusion.4
  143.1 3.2 convolution_convert_fusion.1
  146.4 1.7 constant_dynamic-slice_fusion.5
  148.1 1.6 copy.71
  151.5 4.9 %collective-permute-done.36.refs_4_ = bf16[2,2,2,96,384]{4,3,2,1,0:T(8,128)(2,1)S(1)} collective-permute-done((bf16[2,2,2,96,384]{4,3,2,1,0:T(8,128)(2,1)S(1)}, bf16[2,2,2,96,384]{4,3,2,1,0:T(8,128)(2,1)S(1)}, u32[]{:S(2)}, u32[]{:S(2)}) %collective-permute-start.36) | collective-permute-done | bytes 589856 | tf_op jit(solution)/shard_map/ppermute | solution.py:336
  158.0 2.4 place.5
  160.5 3.0 fusion.17
  163.4 3.4 %fusion.12 = bf16[288,3072]{1,0:T(8,128)(2,1)S(1)} fusion(f32[288,3072]{1,0:T(8,128)S(1)} %copy-done.50, bf16[288,768]{1,0:T(8,128)(2,1)S(1)} %copy-done.31, bf16[3072,768]{1,0:T(8,128)(2,1)S(1)} %bitcast.249), kind=kOutput, calls=%fused_computation.20 | convolution fusion | flops 1376649216 | bytes 10469376 | tf_op jit(solution)/shard_map/dot_general | solution.py:42
  166.8 2.4 fusion.1
  170.3 1.7 collective-permute-start.41
  172.0 3.2 convolution_convert_fusion
  176.6 1.7 multiply_reduce_fusion.3
  180.4 1.8 convolution_convert_fusion.4
  182.2 2.9 collective-permute-done.40
  188.2 1.6 collective-permute-start.43
  191.3 13.9 %attend_back.1 = (bf16[288,768]{1,0:T(8,128)(2,1)S(1)}, bf16[960,768]{1,0:T(8,128)(2,1)S(1)}, bf16[960,768]{1,0:T(8,128)(2,1)S(1)}) custom-call(s32[3]{0:T(128)S(1)} %clamp_multiply_fusion.starts, bf16[288,768]{1,0:T(8,128)(2,1)S(1)} %copy-done.12, bf16[960,768]{1,0:T(8,128)(2,1)S(1)} %copy-done.7, bf16[960,768]{1,0:T(8,128)(2,1)S(1)} %copy-done.5, ...), custom_call_target="tpu_custom_call" | custom-call | flops 7000000000 | bytes 14000000 | tf_op jit(solution)/shard_map/attend_back/pallas_call | solution.py:607
  210.2 2.9 convolution_convert_fusion.3
  213.2 5.8 %fusion.78 = (bf16[960,768]{1,0:T(8,128)(2,1)S(1)}, f32[768]{0:T(1024)S(1)}, f32[960,768]{1,0:T(8,128)S(1)}, f32[960,768]{1,0:T(8,128)}) fusion(f32[960]{0:T(1024)S(1)} %copy-done.40, bf16[288,768]{1,0:T(8,128)(2,1)} %pad_maximum_fusion.12, bf16[288,768]{1,0:T(8,128)(2,1)} %collective-permute-done.18, bf16[288,768]{1,0:T(8,128)(2,1)} %collective-permute-done.19, ...), kind=kOutput, calls=%fused_computation.246 | convolution fusion | flops 2274508032 | bytes 14168064 | tf_op jit(solution)/shard_map/dot_general | solution.py:42
  223.1 1.6 collective-permute-start.53
  224.8 1.9 convolution_convert_fusion.5
  233.5 1.8 dynamic-slice_bitcast_fusion.6
  238.6 3.3 %collective-permute-start.55 = (bf16[2,24,6144]{2,1,0:T(8,128)(2,1)S(1)}, bf16[2,24,6144]{2,1,0:T(8,128)(2,1)S(1)}, u32[]{:S(2)}, u32[]{:S(2)}) collective-permute-start(bf16[2,24,6144]{2,1,0:T(8,128)(2,1)S(1)} %dynamic-slice_bitcast_fusion.3), channel_id=1, source_target_pairs={{0,2},{1,3},{2,0},{3,1},{4,6},{5,7},{6,4},{7,5},{8,10},{9,11},{10,... | collective-permute-start | bytes 1769480 | tf_op jit(solution)/shard_map/ppermute | solution.py:340
  244.4 20.1 %collective-permute-done.55 = bf16[2,24,6144]{2,1,0:T(8,128)(2,1)S(1)} collective-permute-done((bf16[2,24,6144]{2,1,0:T(8,128)(2,1)S(1)}, bf16[2,24,6144]{2,1,0:T(8,128)(2,1)S(1)}, u32[]{:S(2)}, u32[]{:S(2)}) %collective-permute-start.55) | collective-permute-done | bytes 589856 | tf_op jit(solution)/shard_map/ppermute | solution.py:340
  264.8 12.4 %collective-permute-done.49 = bf16[2,4,24,1664]{3,2,1,0:T(8,128)(2,1)S(1)} collective-permute-done((bf16[2,4,24,1664]{3,2,1,0:T(8,128)(2,1)S(1)}, bf16[2,4,24,1664]{3,2,1,0:T(8,128)(2,1)S(1)}, u32[]{:S(2)}, u32[]{:S(2)}) %collective-permute-start.49) | collective-permute-done | bytes 639008 | tf_op jit(solution)/shard_map/ppermute | solution.py:340
  277.4 1.6 multiply_reduce_fusion.2
  281.1 5.5 %collective-permute-start.58 = (bf16[192,768]{1,0:T(8,128)(2,1)S(1)}, bf16[192,768]{1,0:T(8,128)(2,1)S(1)}, u32[]{:S(2)}, u32[]{:S(2)}) collective-permute-start(bf16[192,768]{1,0:T(8,128)(2,1)S(1)} %bitcast.274), channel_id=1, source_target_pairs={{0,2},{1,5},{2,0},{3,3},{4,6},{5,1},{6,4},{7,7},{8,10},{9,13},{10,... | collective-permute-start | bytes 884744 | tf_op jit(solution)/shard_map/ppermute | solution.py:340
  286.7 2.3 collective-permute-start.57
  288.9 11.0 %collective-permute-done.64 = bf16[24,6144]{1,0:T(8,128)(2,1)S(1)} collective-permute-done((bf16[24,6144]{1,0:T(8,128)(2,1)S(1)}, bf16[24,6144]{1,0:T(8,128)(2,1)S(1)}, u32[]{:S(2)}, u32[]{:S(2)}) %collective-permute-start.64) | collective-permute-done | bytes 294944 | tf_op jit(solution)/shard_map/ppermute | solution.py:340
  301.3 1.8 collective-permute-done.57
  305.2 2.8 collective-permute-done.60
  308.3 3.0 collective-permute-start.62
  313.6 3.4 %collective-permute-done.61 = bf16[24,3200]{1,0:T(8,128)(2,1)S(1)} collective-permute-done((bf16[24,3200]{1,0:T(8,128)(2,1)S(1)}, bf16[24,3200]{1,0:T(8,128)(2,1)S(1)}, u32[]{:S(2)}, u32[]{:S(2)}) %collective-permute-start.61) | collective-permute-done | bytes 153632 | tf_op jit(solution)/shard_map/ppermute | solution.py:340
  317.0 3.5 %collective-permute-done.62 = bf16[24,3200]{1,0:T(8,128)(2,1)S(1)} collective-permute-done((bf16[24,3200]{1,0:T(8,128)(2,1)S(1)}, bf16[24,3200]{1,0:T(8,128)(2,1)S(1)}, u32[]{:S(2)}, u32[]{:S(2)}) %collective-permute-start.62) | collective-permute-done | bytes 153632 | tf_op jit(solution)/shard_map/ppermute | solution.py:340
  (339 shorter events, 73.7 us)
Async XLA Ops:
  2.4 16.6 %collective-permute-start.4 = (bf16[24,2432]{1,0:T(8,128)(2,1)S(1)}, bf16[24,2432]{1,0:T(8,128)(2,1)S(1)}, u32[]{:S(2)}, u32[]{:S(2)}) collective-permute-start(bf16[24,2432]{1,0:T(8,128)(2,1)S(1)} %get-tuple-element.228), channel_id=1, source_target_pairs={{0,4},{1,5},{2,6},{3,7},{4,0},{5,1},{6,2},{7,3},{8,12},{9,13},{10,... | collective-permute-start | bytes 350216 | tf_op jit(solution)/shard_map/ppermute | solution.py:340
  7.7 19.2 %collective-permute-start.3 = (bf16[96,768]{1,0:T(8,128)(2,1)S(1)}, bf16[96,768]{1,0:T(8,128)(2,1)S(1)}, u32[]{:S(2)}, u32[]{:S(2)}) collective-permute-start(bf16[96,768]{1,0:T(8,128)(2,1)S(1)} %get-tuple-element.213), channel_id=1, source_target_pairs={{0,5},{8,13},{16,21},{24,29}} | collective-permute-start | bytes 442376 | tf_op jit(solution)/shard_map/ppermute | solution.py:340
  10.9 16.0 %collective-permute-start.2 = (bf16[96,768]{1,0:T(8,128)(2,1)S(1)}, bf16[96,768]{1,0:T(8,128)(2,1)S(1)}, u32[]{:S(2)}, u32[]{:S(2)}) collective-permute-start(bf16[96,768]{1,0:T(8,128)(2,1)S(1)} %get-tuple-element.214), channel_id=1, source_target_pairs={{2,0},{5,1},{0,2},{3,3},{6,4},{1,5},{4,6},{7,7},{10,8},{13,9},{8,1... | collective-permute-start | bytes 442376 | tf_op jit(solution)/shard_map/ppermute | solution.py:340
  12.8 14.1 %collective-permute-start = (bf16[96,768]{1,0:T(8,128)(2,1)S(1)}, bf16[96,768]{1,0:T(8,128)(2,1)S(1)}, u32[]{:S(2)}, u32[]{:S(2)}) collective-permute-start(bf16[96,768]{1,0:T(8,128)(2,1)S(1)} %get-tuple-element.215), channel_id=1, source_target_pairs={{0,0},{3,1},{6,2},{1,3},{4,4},{7,5},{2,6},{5,7},{8,8},{11,9},{14,1... | collective-permute-start | bytes 442376 | tf_op jit(solution)/shard_map/ppermute | solution.py:340
  13.5 13.4 %collective-permute-start.1 = (bf16[96,768]{1,0:T(8,128)(2,1)S(1)}, bf16[96,768]{1,0:T(8,128)(2,1)S(1)}, u32[]{:S(2)}, u32[]{:S(2)}) collective-permute-start(bf16[96,768]{1,0:T(8,128)(2,1)S(1)} %get-tuple-element.216), channel_id=1, source_target_pairs={{1,0},{4,1},{7,2},{2,3},{5,4},{0,5},{3,6},{6,7},{9,8},{12,9},{15,1... | collective-permute-start | bytes 442376 | tf_op jit(solution)/shard_map/ppermute | solution.py:340
  19.0 7.8 %collective-permute-start.5 = (bf16[2,24,2432]{2,1,0:T(8,128)(2,1)S(1)}, bf16[2,24,2432]{2,1,0:T(8,128)(2,1)S(1)}, u32[]{:S(2)}, u32[]{:S(2)}) collective-permute-start(bf16[2,24,2432]{2,1,0:T(8,128)(2,1)S(1)} %get-tuple-element.224), channel_id=1, source_target_pairs={{0,2},{1,3},{2,0},{3,1},{4,6},{5,7},{6,4},{7,5},{8,10},{9,11},{10,... | collective-permute-start | bytes 700424 | tf_op jit(solution)/shard_map/ppermute | solution.py:340
  27.0 10.0 %collective-permute-start.8 = (bf16[24,3840]{1,0:T(8,128)(2,1)S(1)}, bf16[24,3840]{1,0:T(8,128)(2,1)S(1)}, u32[]{:S(2)}, u32[]{:S(2)}) collective-permute-start(bf16[24,3840]{1,0:T(8,128)(2,1)S(1)} %fusion.51), channel_id=1, source_target_pairs={{0,4},{1,5},{2,6},{3,7},{4,0},{5,1},{6,2},{7,3},{8,12},{9,13},{10,... | collective-permute-start | bytes 552968 | tf_op jit(solution)/shard_map/ppermute | solution.py:340
  28.0 9.0 %collective-permute-start.7 = (bf16[2,2,24,1152]{3,2,1,0:T(8,128)(2,1)S(1)}, bf16[2,2,24,1152]{3,2,1,0:T(8,128)(2,1)S(1)}, u32[]{:S(2)}, u32[]{:S(2)}) collective-permute-start(bf16[2,2,24,1152]{3,2,1,0:T(8,128)(2,1)S(1)} %get-tuple-element.207), channel_id=1, source_target_pairs={{0,1},{1,0},{2,3},{3,2},{4,5},{5,4},{6,7},{7,6},{8,9},{9,8},{10,11... | collective-permute-start | bytes 663560 | tf_op jit(solution)/shard_map/ppermute | solution.py:340
  30.2 6.9 %collective-permute-start.6 = (bf16[2,2,24,1280]{3,2,1,0:T(8,128)(2,1)S(1)}, bf16[2,2,24,1280]{3,2,1,0:T(8,128)(2,1)S(1)}, u32[]{:S(2)}, u32[]{:S(2)}) collective-permute-start(bf16[2,2,24,1280]{3,2,1,0:T(8,128)(2,1)S(1)} %get-tuple-element.209), channel_id=1, source_target_pairs={{0,16},{8,24},{16,0},{24,8},{1,17},{9,25},{17,1},{25,9},{2,18},{10... | collective-permute-start | bytes 737288 | tf_op jit(solution)/shard_map/ppermute | solution.py:336
  37.1 9.8 %collective-permute-start.9 = (bf16[2,24,3840]{2,1,0:T(8,128)(2,1)S(1)}, bf16[2,24,3840]{2,1,0:T(8,128)(2,1)S(1)}, u32[]{:S(2)}, u32[]{:S(2)}) collective-permute-start(bf16[2,24,3840]{2,1,0:T(8,128)(2,1)S(1)} %pad_maximum_fusion.13), channel_id=1, source_target_pairs={{0,2},{1,3},{2,0},{3,1},{4,6},{5,7},{6,4},{7,5},{8,10},{9,11},{10,... | collective-permute-start | bytes 1105928 | tf_op jit(solution)/shard_map/ppermute | solution.py:340
  39.4 15.0 %collective-permute-start.10 = (bf16[2,2,2,24,1280]{4,3,2,1,0:T(8,128)(2,1)S(1)}, bf16[2,2,2,24,1280]{4,3,2,1,0:T(8,128)(2,1)}, u32[]{:S(2)}, u32[]{:S(2)}) collective-permute-start(bf16[2,2,2,24,1280]{4,3,2,1,0:T(8,128)(2,1)S(1)} %pad_maximum_fusion.9.refs_0_), channel_id=1, source_target_pairs={{0,1},{1,0},{2,3},{3,2},{4,5},{5,4},{6,7},{7,6},{8,9},{9,8},{10,11... | collective-permute-start | bytes 1474568 | tf_op jit(solution)/shard_map/ppermute | solution.py:340
  40.6 26.2 %collective-permute-start.30 = (bf16[96,768]{1,0:T(8,128)(2,1)}, bf16[96,768]{1,0:T(8,128)(2,1)}, u32[]{:S(2)}, u32[]{:S(2)}) collective-permute-start(bf16[96,768]{1,0:T(8,128)(2,1)} %get-tuple-element.212), channel_id=1, source_target_pairs={{0,0},{3,1},{6,2},{1,3},{4,4},{7,5},{2,6},{5,7},{8,8},{11,9},{14,1... | collective-permute-start | bytes 442376 | tf_op jit(solution)/shard_map/ppermute | solution.py:340
  43.4 11.0 %collective-permute-start.11 = (bf16[2,2,2,24,1152]{4,3,2,1,0:T(8,128)(2,1)S(1)}, bf16[2,2,2,24,1152]{4,3,2,1,0:T(8,128)(2,1)}, u32[]{:S(2)}, u32[]{:S(2)}) collective-permute-start(bf16[2,2,2,24,1152]{4,3,2,1,0:T(8,128)(2,1)S(1)} %pad_maximum_fusion.11.refs_1_), channel_id=1, source_target_pairs={{0,16},{8,24},{16,0},{24,8},{1,17},{9,25},{17,1},{25,9},{2,18},{10... | collective-permute-start | bytes 1327112 | tf_op jit(solution)/shard_map/ppermute | solution.py:336
  55.3 14.1 %collective-permute-start.16 = (bf16[2,2,24,1920]{3,2,1,0:T(8,128)(2,1)}, bf16[2,2,24,1920]{3,2,1,0:T(8,128)(2,1)S(1)}, u32[]{:S(2)}, u32[]{:S(2)}) collective-permute-start(bf16[2,2,24,1920]{3,2,1,0:T(8,128)(2,1)} %get-tuple-element.193), channel_id=1, source_target_pairs={{0,1},{1,0},{2,3},{3,2},{4,5},{5,4},{6,7},{7,6},{8,9},{9,8},{10,11... | collective-permute-start | bytes 1105928 | tf_op jit(solution)/shard_map/ppermute | solution.py:340
  56.3 12.9 %collective-permute-start.12 = (bf16[96,768]{1,0:T(8,128)(2,1)S(1)}, bf16[96,768]{1,0:T(8,128)(2,1)S(1)}, u32[]{:S(2)}, u32[]{:S(2)}) collective-permute-start(bf16[96,768]{1,0:T(8,128)(2,1)S(1)} %pad.34), channel_id=1, source_target_pairs={{0,4},{1,5},{2,6},{3,7},{4,0},{5,1},{6,2},{7,3},{8,12},{9,13},{10,... | collective-permute-start | bytes 442376 | tf_op jit(solution)/shard_map/ppermute | solution.py:340
  60.5 10.2 %collective-permute-start.32 = (bf16[96,768]{1,0:T(8,128)(2,1)}, bf16[96,768]{1,0:T(8,128)(2,1)S(1)}, u32[]{:S(2)}, u32[]{:S(2)}) collective-permute-start(bf16[96,768]{1,0:T(8,128)(2,1)} %get-tuple-element.210), channel_id=1, source_target_pairs={{2,0},{5,1},{0,2},{3,3},{6,4},{1,5},{4,6},{7,7},{10,8},{13,9},{8,1... | collective-permute-start | bytes 442376 | tf_op jit(solution)/shard_map/ppermute | solution.py:340
  63.6 7.1 %collective-permute-start.31 = (bf16[96,768]{1,0:T(8,128)(2,1)}, bf16[96,768]{1,0:T(8,128)(2,1)S(1)}, u32[]{:S(2)}, u32[]{:S(2)}) collective-permute-start(bf16[96,768]{1,0:T(8,128)(2,1)} %get-tuple-element.211), channel_id=1, source_target_pairs={{1,0},{4,1},{7,2},{2,3},{5,4},{0,5},{3,6},{6,7},{9,8},{12,9},{15,1... | collective-permute-start | bytes 442376 | tf_op jit(solution)/shard_map/ppermute | solution.py:340
  66.8 7.9 %collective-permute-start.14 = (bf16[2,2,24,1920]{3,2,1,0:T(8,128)(2,1)S(1)}, bf16[2,2,24,1920]{3,2,1,0:T(8,128)(2,1)S(1)}, u32[]{:S(2)}, u32[]{:S(2)}) collective-permute-start(bf16[2,2,24,1920]{3,2,1,0:T(8,128)(2,1)S(1)} %get-tuple-element.194), channel_id=1, source_target_pairs={{0,16},{8,24},{16,0},{24,8},{1,17},{9,25},{17,1},{25,9},{2,18},{10... | collective-permute-start | bytes 1105928 | tf_op jit(solution)/shard_map/ppermute | solution.py:336
  69.4 9.5 %collective-permute-start.13 = (bf16[2,96,768]{2,1,0:T(8,128)(2,1)S(1)}, bf16[2,96,768]{2,1,0:T(8,128)(2,1)S(1)}, u32[]{:S(2)}, u32[]{:S(2)}) collective-permute-start(bf16[2,96,768]{2,1,0:T(8,128)(2,1)S(1)} %get-tuple-element.222), channel_id=1, source_target_pairs={{0,2},{1,3},{2,0},{3,1},{4,6},{5,7},{6,4},{7,5},{8,10},{9,11},{10,... | collective-permute-start | bytes 884744 | tf_op jit(solution)/shard_map/ppermute | solution.py:340
  70.7 9.7 %collective-permute-start.20 = (bf16[2,2,2,24,1280]{4,3,2,1,0:T(8,128)(2,1)S(1)}, bf16[2,2,2,24,1280]{4,3,2,1,0:T(8,128)(2,1)S(1)}, u32[]{:S(2)}, u32[]{:S(2)}) collective-permute-start(bf16[2,2,2,24,1280]{4,3,2,1,0:T(8,128)(2,1)S(1)} %pad_maximum_fusion.9.refs_0_), channel_id=1, source_target_pairs={{0,8},{8,0},{16,24},{24,16},{1,9},{9,1},{17,25},{25,17},{2,10},{10... | collective-permute-start | bytes 1474568 | tf_op jit(solution)/shard_map/ppermute | solution.py:336
  70.7 13.0 %collective-permute-start.23 = (bf16[2,2,2,24,1152]{4,3,2,1,0:T(8,128)(2,1)}, bf16[2,2,2,24,1152]{4,3,2,1,0:T(8,128)(2,1)S(1)}, u32[]{:S(2)}, u32[]{:S(2)}) collective-permute-start(bf16[2,2,2,24,1152]{4,3,2,1,0:T(8,128)(2,1)} %collective-permute-done.11.refs_3_), channel_id=1, source_target_pairs={{0,8},{8,0},{16,24},{24,16},{1,9},{9,1},{17,25},{25,17},{2,10},{10... | collective-permute-start | bytes 1327112 | tf_op jit(solution)/shard_map/ppermute | solution.py:336
  74.7 11.3 %collective-permute-start.22 = (bf16[2,2,2,24,1280]{4,3,2,1,0:T(8,128)(2,1)}, bf16[2,2,2,24,1280]{4,3,2,1,0:T(8,128)(2,1)S(1)}, u32[]{:S(2)}, u32[]{:S(2)}) collective-permute-start(bf16[2,2,2,24,1280]{4,3,2,1,0:T(8,128)(2,1)} %collective-permute-done.10.refs_2_), channel_id=1, source_target_pairs={{0,8},{8,0},{16,24},{24,16},{1,9},{9,1},{17,25},{25,17},{2,10},{10... | collective-permute-start | bytes 1474568 | tf_op jit(solution)/shard_map/ppermute | solution.py:336
  74.8 26.4 %collective-permute-start.15 = (bf16[2,2,2,24,1920]{4,3,2,1,0:T(8,128)(2,1)S(1)}, bf16[2,2,2,24,1920]{4,3,2,1,0:T(8,128)(2,1)S(1)}, u32[]{:S(2)}, u32[]{:S(2)}) collective-permute-start(bf16[2,2,2,24,1920]{4,3,2,1,0:T(8,128)(2,1)S(1)} %pad_maximum_fusion.3.refs_0_), channel_id=1, source_target_pairs={{0,1},{1,0},{2,3},{3,2},{4,5},{5,4},{6,7},{7,6},{8,9},{9,8},{10,11... | collective-permute-start | bytes 2211848 | tf_op jit(solution)/shard_map/ppermute | solution.py:340
  78.8 22.3 %collective-permute-start.17 = (bf16[2,2,2,24,1920]{4,3,2,1,0:T(8,128)(2,1)S(1)}, bf16[2,2,2,24,1920]{4,3,2,1,0:T(8,128)(2,1)}, u32[]{:S(2)}, u32[]{:S(2)}) collective-permute-start(bf16[2,2,2,24,1920]{4,3,2,1,0:T(8,128)(2,1)S(1)} %pad_maximum_fusion.4.refs_1_), channel_id=1, source_target_pairs={{0,16},{8,24},{16,0},{24,8},{1,17},{9,25},{17,1},{25,9},{2,18},{10... | collective-permute-start | bytes 2211848 | tf_op jit(solution)/shard_map/ppermute | solution.py:336
  80.4 11.9 %collective-permute-start.19 = (bf16[288,768]{1,0:T(8,128)(2,1)}, bf16[288,768]{1,0:T(8,128)(2,1)}, u32[]{:S(2)}, u32[]{:S(2)}) collective-permute-start(bf16[288,768]{1,0:T(8,128)(2,1)} %pad_maximum_fusion.12), channel_id=1, source_target_pairs={{0,2},{2,4},{3,5},{5,7},{8,10},{10,12},{11,13},{13,15},{16,18},{18... | collective-permute-start | bytes 1327112 | tf_op jit(solution)/shard_map/ppermute | solution.py:340
  83.6 17.5 %collective-permute-start.18 = (bf16[288,768]{1,0:T(8,128)(2,1)}, bf16[288,768]{1,0:T(8,128)(2,1)}, u32[]{:S(2)}, u32[]{:S(2)}) collective-permute-start(bf16[288,768]{1,0:T(8,128)(2,1)} %pad_maximum_fusion.12), channel_id=1, source_target_pairs={{0,1},{1,2},{2,3},{3,4},{4,5},{5,6},{6,7},{8,9},{9,10},{10,11},{11... | collective-permute-start | bytes 1327112 | tf_op jit(solution)/shard_map/ppermute | solution.py:340
  86.1 35.3 %collective-permute-start.26 = (bf16[2,2,2,24,1920]{4,3,2,1,0:T(8,128)(2,1)S(1)}, bf16[2,2,2,24,1920]{4,3,2,1,0:T(8,128)(2,1)}, u32[]{:S(2)}, u32[]{:S(2)}) collective-permute-start(bf16[2,2,2,24,1920]{4,3,2,1,0:T(8,128)(2,1)S(1)} %pad_maximum_fusion.3.refs_0_), channel_id=1, source_target_pairs={{0,8},{8,0},{16,24},{24,16},{1,9},{9,1},{17,25},{25,17},{2,10},{10... | collective-permute-start | bytes 2211848 | tf_op jit(solution)/shard_map/ppermute | solution.py:336
  92.3 29.1 %collective-permute-start.27 = (bf16[2,2,2,24,1920]{4,3,2,1,0:T(8,128)(2,1)S(1)}, bf16[2,2,2,24,1920]{4,3,2,1,0:T(8,128)(2,1)S(1)}, u32[]{:S(2)}, u32[]{:S(2)}) collective-permute-start(bf16[2,2,2,24,1920]{4,3,2,1,0:T(8,128)(2,1)S(1)} %pad_maximum_fusion.4.refs_1_), channel_id=1, source_target_pairs={{0,8},{8,0},{16,24},{24,16},{1,9},{9,1},{17,25},{25,17},{2,10},{10... | collective-permute-start | bytes 2211848 | tf_op jit(solution)/shard_map/ppermute | solution.py:336
  102.4 10.0 %collective-permute-start.25 = (bf16[2,2,96,384]{3,2,1,0:T(8,128)(2,1)S(1)}, bf16[2,2,96,384]{3,2,1,0:T(8,128)(2,1)S(1)}, u32[]{:S(2)}, u32[]{:S(2)}) collective-permute-start(bf16[2,2,96,384]{3,2,1,0:T(8,128)(2,1)S(1)} %get-tuple-element.204), channel_id=1, source_target_pairs={{0,1},{1,0},{2,3},{3,2},{4,5},{5,4},{6,7},{7,6},{8,9},{9,8},{10,11... | collective-permute-start | bytes 884744 | tf_op jit(solution)/shard_map/ppermute | solution.py:340
  104.9 16.5 %collective-permute-start.28 = (bf16[2,2,2,24,1920]{4,3,2,1,0:T(8,128)(2,1)S(1)}, bf16[2,2,2,24,1920]{4,3,2,1,0:T(8,128)(2,1)S(1)}, u32[]{:S(2)}, u32[]{:S(2)}) collective-permute-start(bf16[2,2,2,24,1920]{4,3,2,1,0:T(8,128)(2,1)S(1)} %collective-permute-done.15.refs_2_), channel_id=1, source_target_pairs={{0,8},{8,0},{16,24},{24,16},{1,9},{9,1},{17,25},{25,17},{2,10},{10... | collective-permute-start | bytes 2211848 | tf_op jit(solution)/shard_map/ppermute | solution.py:336
  104.9 16.5 %collective-permute-start.29 = (bf16[2,2,2,24,1920]{4,3,2,1,0:T(8,128)(2,1)}, bf16[2,2,2,24,1920]{4,3,2,1,0:T(8,128)(2,1)S(1)}, u32[]{:S(2)}, u32[]{:S(2)}) collective-permute-start(bf16[2,2,2,24,1920]{4,3,2,1,0:T(8,128)(2,1)} %collective-permute-done.17.refs_3_), channel_id=1, source_target_pairs={{0,8},{8,0},{16,24},{24,16},{1,9},{9,1},{17,25},{25,17},{2,10},{10... | collective-permute-start | bytes 2211848 | tf_op jit(solution)/shard_map/ppermute | solution.py:336
  112.3 9.0 %collective-permute-start.24 = (bf16[2,2,96,384]{3,2,1,0:T(8,128)(2,1)S(1)}, bf16[2,2,96,384]{3,2,1,0:T(8,128)(2,1)S(1)}, u32[]{:S(2)}, u32[]{:S(2)}) collective-permute-start(bf16[2,2,96,384]{3,2,1,0:T(8,128)(2,1)S(1)} %get-tuple-element.205), channel_id=1, source_target_pairs={{0,16},{8,24},{16,0},{24,8},{1,17},{9,25},{17,1},{25,9},{2,18},{10... | collective-permute-start | bytes 884744 | tf_op jit(solution)/shard_map/ppermute | solution.py:336
  121.5 28.8 %collective-permute-start.34 = (bf16[2,2,2,96,384]{4,3,2,1,0:T(8,128)(2,1)S(1)}, bf16[2,2,2,96,384]{4,3,2,1,0:T(8,128)(2,1)}, u32[]{:S(2)}, u32[]{:S(2)}) collective-permute-start(bf16[2,2,2,96,384]{4,3,2,1,0:T(8,128)(2,1)S(1)} %pad_maximum_fusion.6.refs_0_), channel_id=1, source_target_pairs={{0,1},{1,0},{2,3},{3,2},{4,5},{5,4},{6,7},{7,6},{8,9},{9,8},{10,11... | collective-permute-start | bytes 1769480 | tf_op jit(solution)/shard_map/ppermute | solution.py:340
  121.9 28.9 %collective-permute-start.35 = (bf16[2,2,2,96,384]{4,3,2,1,0:T(8,128)(2,1)S(1)}, bf16[2,2,2,96,384]{4,3,2,1,0:T(8,128)(2,1)}, u32[]{:S(2)}, u32[]{:S(2)}) collective-permute-start(bf16[2,2,2,96,384]{4,3,2,1,0:T(8,128)(2,1)S(1)} %pad_maximum_fusion.7.refs_1_), channel_id=1, source_target_pairs={{0,16},{8,24},{16,0},{24,8},{1,17},{9,25},{17,1},{25,9},{2,18},{10... | collective-permute-start | bytes 1769480 | tf_op jit(solution)/shard_map/ppermute | solution.py:336
  149.8 17.1 %collective-permute-start.33 = (bf16[2,4,2,96,768]{4,3,1,0,2:T(8,128)(2,1)}, bf16[2,4,2,96,768]{4,3,1,0,2:T(8,128)(2,1)}, u32[]{:S(2)}, u32[]{:S(2)}) collective-permute-start(bf16[2,4,2,96,768]{4,3,1,0,2:T(8,128)(2,1)} %bitcast.235), channel_id=1, source_target_pairs={{0,8},{8,0},{16,24},{24,16},{1,9},{9,1},{17,25},{25,17},{2,10},{10... | collective-permute-start | bytes 7077896 | tf_op jit(solution)/shard_map/ppermute | solution.py:336
  149.8 6.7 %collective-permute-start.36 = (bf16[2,2,2,96,384]{4,3,2,1,0:T(8,128)(2,1)S(1)}, bf16[2,2,2,96,384]{4,3,2,1,0:T(8,128)(2,1)S(1)}, u32[]{:S(2)}, u32[]{:S(2)}) collective-permute-start(bf16[2,2,2,96,384]{4,3,2,1,0:T(8,128)(2,1)S(1)} %pad_maximum_fusion.6.refs_0_), channel_id=1, source_target_pairs={{0,8},{8,0},{16,24},{24,16},{1,9},{9,1},{17,25},{25,17},{2,10},{10... | collective-permute-start | bytes 1769480 | tf_op jit(solution)/shard_map/ppermute | solution.py:336
  150.3 7.0 %collective-permute-start.37 = (bf16[2,2,2,96,384]{4,3,2,1,0:T(8,128)(2,1)S(1)}, bf16[2,2,2,96,384]{4,3,2,1,0:T(8,128)(2,1)S(1)}, u32[]{:S(2)}, u32[]{:S(2)}) collective-permute-start(bf16[2,2,2,96,384]{4,3,2,1,0:T(8,128)(2,1)S(1)} %pad_maximum_fusion.7.refs_1_), channel_id=1, source_target_pairs={{0,8},{8,0},{16,24},{24,16},{1,9},{9,1},{17,25},{25,17},{2,10},{10... | collective-permute-start | bytes 1769480 | tf_op jit(solution)/shard_map/ppermute | solution.py:336
  150.3 7.0 %collective-permute-start.38 = (bf16[2,2,2,96,384]{4,3,2,1,0:T(8,128)(2,1)}, bf16[2,2,2,96,384]{4,3,2,1,0:T(8,128)(2,1)S(1)}, u32[]{:S(2)}, u32[]{:S(2)}) collective-permute-start(bf16[2,2,2,96,384]{4,3,2,1,0:T(8,128)(2,1)} %collective-permute-done.34.refs_2_), channel_id=1, source_target_pairs={{0,8},{8,0},{16,24},{24,16},{1,9},{9,1},{17,25},{25,17},{2,10},{10... | collective-permute-start | bytes 1769480 | tf_op jit(solution)/shard_map/ppermute | solution.py:336
  150.8 7.2 %collective-permute-start.39 = (bf16[2,2,2,96,384]{4,3,2,1,0:T(8,128)(2,1)}, bf16[2,2,2,96,384]{4,3,2,1,0:T(8,128)(2,1)}, u32[]{:S(2)}, u32[]{:S(2)}) collective-permute-start(bf16[2,2,2,96,384]{4,3,2,1,0:T(8,128)(2,1)} %collective-permute-done.35.refs_3_), channel_id=1, source_target_pairs={{0,8},{8,0},{16,24},{24,16},{1,9},{9,1},{17,25},{25,17},{2,10},{10... | collective-permute-start | bytes 1769480 | tf_op jit(solution)/shard_map/ppermute | solution.py:336
  169.7 15.4 %collective-permute-start.40 = (bf16[4,2,96,384]{3,2,0,1:T(8,128)(2,1)S(1)}, bf16[4,2,96,384]{3,2,0,1:T(8,128)(2,1)S(1)}, u32[]{:S(2)}, u32[]{:S(2)}) collective-permute-start(bf16[4,2,96,384]{3,2,0,1:T(8,128)(2,1)S(1)} %dynamic-slice_bitcast_fusion.11), channel_id=1, source_target_pairs={{0,16},{8,24},{16,0},{24,8},{1,17},{9,25},{17,1},{25,9},{2,18},{10... | collective-permute-start | bytes 1769480 | tf_op jit(solution)/shard_map/ppermute | solution.py:336
  170.3 15.1 %collective-permute-start.41 = (bf16[2,4,96,384]{3,2,1,0:T(8,128)(2,1)S(1)}, bf16[2,4,96,384]{3,2,1,0:T(8,128)(2,1)S(1)}, u32[]{:S(2)}, u32[]{:S(2)}) collective-permute-start(bf16[2,4,96,384]{3,2,1,0:T(8,128)(2,1)S(1)} %dynamic-slice_bitcast_fusion.10), channel_id=1, source_target_pairs={{0,1},{1,0},{2,3},{3,2},{4,5},{5,4},{6,7},{7,6},{8,9},{9,8},{10,11... | collective-permute-start | bytes 1769480 | tf_op jit(solution)/shard_map/ppermute | solution.py:340
  175.7 10.0 %collective-permute-start.42 = (bf16[2,4,2,24,3072]{4,3,1,0,2:T(8,128)(2,1)S(1)}, bf16[2,4,2,24,3072]{4,3,1,0,2:T(8,128)(2,1)S(1)}, u32[]{:S(2)}, u32[]{:S(2)}) collective-permute-start(bf16[2,4,2,24,3072]{4,3,1,0,2:T(8,128)(2,1)S(1)} %bitcast.257), channel_id=1, source_target_pairs={{0,8},{8,0},{16,24},{24,16},{1,9},{9,1},{17,25},{25,17},{2,10},{10... | collective-permute-start | bytes 7077896 | tf_op jit(solution)/shard_map/ppermute | solution.py:336
  186.7 18.5 %collective-permute-start.44 = (bf16[4,96,384]{2,1,0:T(8,128)(2,1)S(1)}, bf16[4,96,384]{2,1,0:T(8,128)(2,1)S(1)}, u32[]{:S(2)}, u32[]{:S(2)}) collective-permute-start(bf16[4,96,384]{2,1,0:T(8,128)(2,1)S(1)} %dynamic-slice_bitcast_fusion.17), channel_id=1, source_target_pairs={{0,16},{8,24},{16,0},{24,8},{1,17},{9,25},{17,1},{25,9},{2,18},{10... | collective-permute-start | bytes 884744 | tf_op jit(solution)/shard_map/ppermute | solution.py:336
  188.2 17.0 %collective-permute-start.43 = (bf16[4,96,384]{2,1,0:T(8,128)(2,1)S(1)}, bf16[4,96,384]{2,1,0:T(8,128)(2,1)S(1)}, u32[]{:S(2)}, u32[]{:S(2)}) collective-permute-start(bf16[4,96,384]{2,1,0:T(8,128)(2,1)S(1)} %dynamic-slice_bitcast_fusion.18), channel_id=1, source_target_pairs={{0,1},{1,0},{2,3},{3,2},{4,5},{5,4},{6,7},{7,6},{8,9},{9,8},{10,11... | collective-permute-start | bytes 884744 | tf_op jit(solution)/shard_map/ppermute | solution.py:340
  190.2 17.2 %collective-permute-start.45 = (bf16[4,2,24,1536]{3,2,0,1:T(8,128)(2,1)S(1)}, bf16[4,2,24,1536]{3,2,0,1:T(8,128)(2,1)S(1)}, u32[]{:S(2)}, u32[]{:S(2)}) collective-permute-start(bf16[4,2,24,1536]{3,2,0,1:T(8,128)(2,1)S(1)} %dynamic-slice_bitcast_fusion.9), channel_id=1, source_target_pairs={{0,16},{8,24},{16,0},{24,8},{1,17},{9,25},{17,1},{25,9},{2,18},{10... | collective-permute-start | bytes 1769480 | tf_op jit(solution)/shard_map/ppermute | solution.py:336
  190.8 17.7 %collective-permute-start.46 = (bf16[2,4,24,1536]{3,2,1,0:T(8,128)(2,1)S(1)}, bf16[2,4,24,1536]{3,2,1,0:T(8,128)(2,1)S(1)}, u32[]{:S(2)}, u32[]{:S(2)}) collective-permute-start(bf16[2,4,24,1536]{3,2,1,0:T(8,128)(2,1)S(1)} %dynamic-slice_bitcast_fusion.8), channel_id=1, source_target_pairs={{0,1},{1,0},{2,3},{3,2},{4,5},{5,4},{6,7},{7,6},{8,9},{9,8},{10,11... | collective-permute-start | bytes 1769480 | tf_op jit(solution)/shard_map/ppermute | solution.py:340
  222.5 14.9 %collective-permute-start.54 = (bf16[4,24,1536]{2,1,0:T(8,128)(2,1)}, bf16[4,24,1536]{2,1,0:T(8,128)(2,1)}, u32[]{:S(2)}, u32[]{:S(2)}) collective-permute-start(bf16[4,24,1536]{2,1,0:T(8,128)(2,1)} %dynamic-slice_bitcast_fusion.15), channel_id=1, source_target_pairs={{0,16},{8,24},{16,0},{24,8},{1,17},{9,25},{17,1},{25,9},{2,18},{10... | collective-permute-start | bytes 884744 | tf_op jit(solution)/shard_map/ppermute | solution.py:336
  223.1 12.4 %collective-permute-start.53 = (bf16[4,24,1536]{2,1,0:T(8,128)(2,1)}, bf16[4,24,1536]{2,1,0:T(8,128)(2,1)}, u32[]{:S(2)}, u32[]{:S(2)}) collective-permute-start(bf16[4,24,1536]{2,1,0:T(8,128)(2,1)} %dynamic-slice_bitcast_fusion.16), channel_id=1, source_target_pairs={{0,1},{1,0},{2,3},{3,2},{4,5},{5,4},{6,7},{7,6},{8,9},{9,8},{10,11... | collective-permute-start | bytes 884744 | tf_op jit(solution)/shard_map/ppermute | solution.py:340
  228.3 49.0 %collective-permute-start.52 = (bf16[96,768]{1,0:T(8,128)(2,1)}, bf16[96,768]{1,0:T(8,128)(2,1)S(1)}, u32[]{:S(2)}, u32[]{:S(2)}) collective-permute-start(bf16[96,768]{1,0:T(8,128)(2,1)} %slice.248), channel_id=1, source_target_pairs={{5,2},{13,10},{21,18},{29,26}} | collective-permute-start | bytes 442376 | tf_op jit(solution)/shard_map/ppermute | solution.py:340
  230.9 46.5 %collective-permute-start.51 = (bf16[288,768]{1,0:T(8,128)(2,1)}, bf16[288,768]{1,0:T(8,128)(2,1)S(1)}, u32[]{:S(2)}, u32[]{:S(2)}) collective-permute-start(bf16[288,768]{1,0:T(8,128)(2,1)} %get-tuple-element.180), channel_id=1, source_target_pairs={{2,0},{4,2},{5,3},{7,5},{10,8},{12,10},{13,11},{15,13},{18,16},{20... | collective-permute-start | bytes 1327112 | tf_op jit(solution)/shard_map/ppermute | solution.py:340
  232.2 45.2 %collective-permute-start.50 = (bf16[288,768]{1,0:T(8,128)(2,1)}, bf16[288,768]{1,0:T(8,128)(2,1)S(1)}, u32[]{:S(2)}, u32[]{:S(2)}) collective-permute-start(bf16[288,768]{1,0:T(8,128)(2,1)} %get-tuple-element.181), channel_id=1, source_target_pairs={{1,0},{2,1},{3,2},{4,3},{5,4},{6,5},{7,6},{9,8},{10,9},{11,10},{12... | collective-permute-start | bytes 1327112 | tf_op jit(solution)/shard_map/ppermute | solution.py:340
  235.5 6.4 %collective-permute-start.47 = (bf16[2,192,3200]{2,1,0:T(8,128)(2,1)S(1)}, bf16[2,192,3200]{2,1,0:T(8,128)(2,1)S(1)}, u32[]{:S(2)}, u32[]{:S(2)}) collective-permute-start(bf16[2,192,3200]{2,1,0:T(8,128)(2,1)S(1)} %pad_maximum_fusion), channel_id=1, source_target_pairs={{0,8},{8,0},{16,24},{24,16},{1,9},{9,1},{17,25},{25,17},{2,10},{10... | collective-permute-start | bytes 7372808 | tf_op jit(solution)/shard_map/ppermute | solution.py:336
  238.6 25.9 %collective-permute-start.55 = (bf16[2,24,6144]{2,1,0:T(8,128)(2,1)S(1)}, bf16[2,24,6144]{2,1,0:T(8,128)(2,1)S(1)}, u32[]{:S(2)}, u32[]{:S(2)}) collective-permute-start(bf16[2,24,6144]{2,1,0:T(8,128)(2,1)S(1)} %dynamic-slice_bitcast_fusion.3), channel_id=1, source_target_pairs={{0,2},{1,3},{2,0},{3,1},{4,6},{5,7},{6,4},{7,5},{8,10},{9,11},{10,... | collective-permute-start | bytes 1769480 | tf_op jit(solution)/shard_map/ppermute | solution.py:340
  242.9 21.7 %collective-permute-start.48 = (bf16[4,2,24,1536]{3,2,0,1:T(8,128)(2,1)S(1)}, bf16[4,2,24,1536]{3,2,0,1:T(8,128)(2,1)S(1)}, u32[]{:S(2)}, u32[]{:S(2)}) collective-permute-start(bf16[4,2,24,1536]{3,2,0,1:T(8,128)(2,1)S(1)} %bitcast.269), channel_id=1, source_target_pairs={{0,16},{8,24},{16,0},{24,8},{1,17},{9,25},{17,1},{25,9},{2,18},{10... | collective-permute-start | bytes 1769480 | tf_op jit(solution)/shard_map/ppermute | solution.py:336
  264.5 12.7 %collective-permute-start.49 = (bf16[2,4,24,1664]{3,2,1,0:T(8,128)(2,1)S(1)}, bf16[2,4,24,1664]{3,2,1,0:T(8,128)(2,1)S(1)}, u32[]{:S(2)}, u32[]{:S(2)}) collective-permute-start(bf16[2,4,24,1664]{3,2,1,0:T(8,128)(2,1)S(1)} %dynamic-slice_bitcast_fusion.2), channel_id=1, source_target_pairs={{0,1},{1,0},{2,3},{3,2},{4,5},{5,4},{6,7},{7,6},{8,9},{9,8},{10,11... | collective-permute-start | bytes 1916936 | tf_op jit(solution)/shard_map/ppermute | solution.py:340
  279.8 20.1 %collective-permute-start.64 = (bf16[24,6144]{1,0:T(8,128)(2,1)S(1)}, bf16[24,6144]{1,0:T(8,128)(2,1)S(1)}, u32[]{:S(2)}, u32[]{:S(2)}) collective-permute-start(bf16[24,6144]{1,0:T(8,128)(2,1)S(1)} %dynamic-slice_bitcast_fusion.13), channel_id=1, source_target_pairs={{0,4},{1,5},{2,6},{3,7},{4,0},{5,1},{6,2},{7,3},{8,12},{9,13},{10,... | collective-permute-start | bytes 884744 | tf_op jit(solution)/shard_map/ppermute | solution.py:340
  279.8 21.2 %collective-permute-start.59 = (bf16[4,24,1536]{2,1,0:T(8,128)(2,1)S(1)}, bf16[4,24,1536]{2,1,0:T(8,128)(2,1)S(1)}, u32[]{:S(2)}, u32[]{:S(2)}) collective-permute-start(bf16[4,24,1536]{2,1,0:T(8,128)(2,1)S(1)} %dynamic-slice_bitcast_fusion.14), channel_id=1, source_target_pairs={{0,1},{1,0},{2,3},{3,2},{4,5},{5,4},{6,7},{7,6},{8,9},{9,8},{10,11... | collective-permute-start | bytes 884744 | tf_op jit(solution)/shard_map/ppermute | solution.py:340
  280.3 20.9 %collective-permute-start.56 = (bf16[192,768]{1,0:T(8,128)(2,1)S(1)}, bf16[192,768]{1,0:T(8,128)(2,1)S(1)}, u32[]{:S(2)}, u32[]{:S(2)}) collective-permute-start(bf16[192,768]{1,0:T(8,128)(2,1)S(1)} %bitcast.276), channel_id=1, source_target_pairs={{0,0},{1,3},{2,6},{3,1},{4,4},{5,7},{6,2},{7,5},{8,8},{9,11},{10,1... | collective-permute-start | bytes 884744 | tf_op jit(solution)/shard_map/ppermute | solution.py:340
  281.1 22.0 %collective-permute-start.58 = (bf16[192,768]{1,0:T(8,128)(2,1)S(1)}, bf16[192,768]{1,0:T(8,128)(2,1)S(1)}, u32[]{:S(2)}, u32[]{:S(2)}) collective-permute-start(bf16[192,768]{1,0:T(8,128)(2,1)S(1)} %bitcast.274), channel_id=1, source_target_pairs={{0,2},{1,5},{2,0},{3,3},{4,6},{5,1},{6,4},{7,7},{8,10},{9,13},{10,... | collective-permute-start | bytes 884744 | tf_op jit(solution)/shard_map/ppermute | solution.py:340
  286.7 16.5 %collective-permute-start.57 = (bf16[192,768]{1,0:T(8,128)(2,1)S(1)}, bf16[192,768]{1,0:T(8,128)(2,1)S(1)}, u32[]{:S(2)}, u32[]{:S(2)}) collective-permute-start(bf16[192,768]{1,0:T(8,128)(2,1)S(1)} %bitcast.275), channel_id=1, source_target_pairs={{0,1},{1,4},{2,7},{3,2},{4,5},{5,0},{6,3},{7,6},{8,9},{9,12},{10,1... | collective-permute-start | bytes 884744 | tf_op jit(solution)/shard_map/ppermute | solution.py:340
  299.9 8.2 %collective-permute-start.60 = (bf16[4,24,1664]{2,1,0:T(8,128)(2,1)S(1)}, bf16[4,24,1664]{2,1,0:T(8,128)(2,1)S(1)}, u32[]{:S(2)}, u32[]{:S(2)}) collective-permute-start(bf16[4,24,1664]{2,1,0:T(8,128)(2,1)S(1)} %dynamic-slice_bitcast_fusion.12), channel_id=1, source_target_pairs={{0,16},{8,24},{16,0},{24,8},{1,17},{9,25},{17,1},{25,9},{2,18},{10... | collective-permute-start | bytes 958472 | tf_op jit(solution)/shard_map/ppermute | solution.py:336
  308.2 8.8 %collective-permute-start.61 = (bf16[24,3200]{1,0:T(8,128)(2,1)S(1)}, bf16[24,3200]{1,0:T(8,128)(2,1)S(1)}, u32[]{:S(2)}, u32[]{:S(2)}) collective-permute-start(bf16[24,3200]{1,0:T(8,128)(2,1)S(1)} %get-tuple-element.195), channel_id=1, source_target_pairs={{0,2},{1,3},{2,4},{3,5},{4,6},{5,7},{6,0},{7,1},{8,10},{9,11},{10,... | collective-permute-start | bytes 460808 | tf_op jit(solution)/shard_map/ppermute | solution.py:340
  308.3 12.2 %collective-permute-start.62 = (bf16[24,3200]{1,0:T(8,128)(2,1)S(1)}, bf16[24,3200]{1,0:T(8,128)(2,1)S(1)}, u32[]{:S(2)}, u32[]{:S(2)}) collective-permute-start(bf16[24,3200]{1,0:T(8,128)(2,1)S(1)} %get-tuple-element.196), channel_id=1, source_target_pairs={{0,4},{1,5},{2,6},{3,7},{4,0},{5,1},{6,2},{7,3},{8,12},{9,13},{10,... | collective-permute-start | bytes 460808 | tf_op jit(solution)/shard_map/ppermute | solution.py:340
  311.3 9.2 %collective-permute-start.63 = (bf16[24,3200]{1,0:T(8,128)(2,1)S(1)}, bf16[24,3200]{1,0:T(8,128)(2,1)S(1)}, u32[]{:S(2)}, u32[]{:S(2)}) collective-permute-start(bf16[24,3200]{1,0:T(8,128)(2,1)S(1)} %get-tuple-element.197), channel_id=1, source_target_pairs={{0,6},{1,7},{2,0},{3,1},{4,2},{5,3},{6,4},{7,5},{8,14},{9,15},{10,... | collective-permute-start | bytes 460808 | tf_op jit(solution)/shard_map/ppermute | solution.py:340
  (56 other events, 536.4 us)
where the time goes:
time: 328 us; the launch traced here: 323 us
  waiting for transfers between devices  113 us (34%)
  starting transfers between devices  81.5 us (25%)
  matrix products  35.4 us (11%)
  Pallas kernels  34.6 us (11%)
  local copies, waits for them, and re-layouts  30.3 us (9%)
  other arithmetic  25.8 us (8%)
    ppermute x38, waiting for transfers between devices, swap_ctx(): return lax.ppermute(array, 'ctx', pairs)  82.5 us
    ppermute x38, starting transfers between devices, swap_ctx(): return lax.ppermute(array, 'ctx', pairs)  65.2 us
    ppermute x27, waiting for transfers between devices, swap_seq(): return lax.ppermute(array, 'seq', pairs)  30.1 us
    ppermute x27, starting transfers between devices, swap_seq(): return lax.ppermute(array, 'seq', pairs)  16.3 us
    pallas_call x1, Pallas kernels, attend_back(): pl.pallas_call(attend_back_kernel, grid_spec=pltpu.PrefetchScalarGridSpec...  13.9 us
    pallas_call x1, Pallas kernels, attend(): pl.pallas_call(attend_kernel, grid_spec=pltpu.PrefetchScalarGridSpec(num_...  13.1 us
    dot_general x5, matrix products, matmul_left_t(): lax.dot_general(left, right, (((0,), (0,)), ((), ())), preferred_element_...  13 us
    dot_general x5, matrix products, matmul_right_t(): lax.dot_general(left, right, (((1,), (1,)), ((), ())), preferred_element_...  13 us
  transfers between devices with their start and end apart: 65, of which 24 were waited for; matrix products, arithmetic and copies ran while one was open for 20% of the time, Pallas kernels for 11%

commit v1 on v0

--- a/solution.py
+++ b/solution.py
@@ -315,7 +315,7 @@
     return (jnp.stack(outputs), jnp.stack(input_grads)) + tuple(owned)
 
 
-FLAGS = {'deal': 3, 'cut': 1280, 'shift': 1, 'f0': 0, 'f1': 1, 'f2': 1, 'f3': 1, 'f4': 0, 'f5': 1, 'f6': 1, 'f7': 0, 'f8': 0, 'home': 0, 'b0': 1, 'b1': 0, 'b2': 1, 'b3': 1, 'b4': 0, 'b5': 0, 'b6': 1, 'b7': 0, 'outin': 1, 'dz': 0, 'c': 0, 'dxfirst': 0, 'lz': 0, 'ez': 0, 'dfold': 0, 'ufold': 0, 'upfirst': 1}
+FLAGS = {'deal': 3, 'cut': 1280, 'shift': 1, 'f0': 0, 'f1': 1, 'f2': 1, 'f3': 1, 'f4': 0, 'f5': 1, 'f6': 1, 'f7': 0, 'f8': 2, 'home': 0, 'b0': 1, 'b1': 0, 'b2': 1, 'b3': 1, 'b4': 2, 'b5': 0, 'b6': 1, 'b7': 0, 'outin': 1, 'dz': 0, 'c': 1, 'dxfirst': 1, 'lz': 0, 'ez': 1, 'dfold': 0, 'ufold': 0, 'upfirst': 1, 'kvg': 1, 'u2': 1, 'homeg': 2, 'lz2g': 1, 'ab': 1, 'dfar': 0, 'late_result': 1, 'any': 0}
 SLOTS = 10
 LOCAL = 96
 WINDOW = 768
@@ -394,7 +394,7 @@
         copy.wait()
 
 
-def all_rows(own, other, columns, blocks, split, width):
+def all_rows(own, other, columns, blocks, split, width, mark):
     rows = own[0].shape[-2]
     cuts = ([], [])
     for low, high, side in ((0, split, 0), (split, columns + blocks * width, 1)):
@@ -409,7 +409,7 @@
         shapes.append(jax.ShapeDtypeStruct((2, 2, 4, 2, blocks, rows, width), own[0].dtype))
     full = pl.pallas_call(
         functools.partial(place_kernel, cuts),
-        in_specs=[pl.BlockSpec(memory_space=pltpu.HBM)] * 8,
+        in_specs=[pl.BlockSpec(memory_space=pl.ANY if FLAGS["any"] & mark else pltpu.HBM)] * 8,
         out_specs=[pl.BlockSpec(memory_space=pltpu.VMEM)] * len(shapes),
         out_shape=shapes,
         scratch_shapes=[pltpu.SemaphoreType.DMA((32 * (len(cuts[0]) + len(cuts[1])),))],
@@ -694,7 +694,7 @@
     )
     inputs_low = jnp.concatenate(dealt, axis=0)
     near = plane_start(line, early_cut)
-    up_own = after(up_own, line)
+    up_own, line = lax.optimization_barrier((up_own, line))
     up_pair = jnp.stack([up_own, swap_ctx(up_own, Z_FAR)])
     if FLAGS["deal"] == 0:
         grad_rows = [swap_ctx(pick(cotangent_wide, (2 * j + ctx) % 3, 0), DEAL[j]) for j in range(2)]
@@ -707,7 +707,9 @@
     pieces = [*near, *ends]
     others = other_core(pieces)
     up_near = plane_start(up_line, (width + ff) // 2)
-    down_own = after(down_own, up_line)
+    down_own, up_line = lax.optimization_barrier((down_own, up_line))
+    if FLAGS["deal"] == 5:
+        cotangent_wide, up_near = lax.optimization_barrier((cotangent_wide, up_near))
     down_pair = jnp.stack([down_own, swap_ctx(down_own, Z_FAR)])
     below = [None, None]
     if FLAGS["shift"] in (0, 1):
@@ -717,15 +719,19 @@
     up_near, down_pair, others, below, inputs_low, cotangent_wide = meet(
         "f4", up_near, down_pair, others, below, inputs_low, cotangent_wide
     )
-    (first,) = all_rows(pieces, others, early_own.shape[1], 0, early_cut, width)
+    (first,) = all_rows(pieces, others, early_own.shape[1], 0, early_cut, width, 1)
     up_ends = plane_end(*up_near)
     down_line = jnp.stack([down_pair, swap_ctx(down_pair, Z_SWAP)])
+    if FLAGS["deal"] == 6:
+        cotangent_wide, up_ends = lax.optimization_barrier((cotangent_wide, up_ends))
     if FLAGS["shift"] == 2:
         below[0] = swap_ctx(inputs_low, UP[0])
     if FLAGS["shift"] in (1, 2):
         below[1] = swap_ctx(inputs_low, UP[1])
     down_line, up_ends, below, _ = meet("f5", down_line, up_ends, below, first)
-    if FLAGS["deal"] == 3:
+    if FLAGS["deal"] == 4:
+        cotangent_wide, down_line = lax.optimization_barrier((cotangent_wide, down_line))
+    if FLAGS["deal"] in (3, 4, 5, 6):
         grad_rows = deal(cotangent_wide)
     down_near = plane_start(down_line, width // 2)
     up_others = other_core([*up_near, *up_ends])
@@ -748,26 +754,33 @@
     key_normed, key_scale = norm_parts(key_rows)
     norm_keys = (key_normed * gain_one).astype(jnp.bfloat16)
     norm_a = norm_keys[KEYS - ROWS :]
+    if FLAGS["kvg"]:
+        norm_keys, norm_a, down_near = lax.optimization_barrier((norm_keys, norm_a, down_near))
     queries = (matmul(norm_a, q_full).astype(jnp.bfloat16) * SCALE).astype(jnp.bfloat16)
     keys_values = matmul(norm_keys, second).astype(jnp.bfloat16)
     keys, values = keys_values[:, :width], keys_values[:, width:]
     queries, keys, values, down_near, up_others = meet("f6", queries, keys, values, down_near, up_others)
     down_ends = plane_end(*down_near)
+    down_others = other_core(down_near)
     if FLAGS["deal"] == 2:
         grad_rows = deal(cotangent_wide)
     attn, probs = attend(queries, keys, values, starts, key_marks, query_marks)
-    attn, down_ends, up_others, grad_rows = meet("f7", attn, down_ends, up_others, grad_rows)
+    attn, down_ends, up_others, down_others, grad_rows = meet("f7", attn, down_ends, up_others, down_others, grad_rows)
     grad_rows = jnp.concatenate(grad_rows, axis=0)
     down_pieces = [*down_near, *down_ends]
-    down_others = other_core(down_pieces)
-    (out_up_full,) = all_rows([*up_near, *up_ends], up_others, width + ff, 0, (width + ff) // 2, width)
+    down_others = down_others + other_core(down_ends)
+    (out_up_full,) = all_rows([*up_near, *up_ends], up_others, width + ff, 0, (width + ff) // 2, width, 2)
     out_full, up_full = out_up_full[:, :width], out_up_full[:, width:]
     branch = matmul(attn, out_full)
     mixed = inputs + branch
     mixed_normed, mixed_scale = norm_parts(mixed)
-    norm_m, down_others = meet("f8", (mixed_normed * gain_two).astype(jnp.bfloat16), down_others)
-    (down_full,) = all_rows(down_pieces, down_others, width, 0, width // 2, width)
+    norm_m = (mixed_normed * gain_two).astype(jnp.bfloat16)
+    if FLAGS["f8"] == 1:
+        norm_m, down_others = meet("f8", norm_m, down_others)
     pre = matmul(norm_m, up_full)
+    if FLAGS["f8"] == 2:
+        pre, down_others = meet("f8", pre, down_others)
+    (down_full,) = all_rows(down_pieces, down_others, width, 0, width // 2, width, 4)
     act, gelu_pull = jax.vjp(gelu_tanh, pre)
     act = act.astype(jnp.bfloat16)
 
@@ -775,14 +788,12 @@
         down_got = fold_send(act, grad_rows)
     else:
         grad_down = matmul_left_t(act, grad_rows).astype(jnp.bfloat16)
-        grad_rows = after(grad_rows, grad_down)
+        grad_rows, grad_down = lax.optimization_barrier((grad_rows, grad_down))
         down_got = fold_part(grad_down)
     grad_pre = gelu_pull(matmul_right_t(grad_rows, down_full))[0].astype(jnp.bfloat16)
-    result_delta = (branch + matmul(act, down_full)).astype(jnp.bfloat16)
-    deltas = result_delta.reshape(3, local_len, width)
-    home = []
-    if FLAGS["home"] == 1:
-        home = send_home(result_delta)
+    if not FLAGS["late_result"]:
+        result_delta = (branch + matmul(act, down_full)).astype(jnp.bfloat16)
+    home, deltas = [], []
     down_got, grad_pre = meet("b0", down_got, grad_pre)
     down_near = fold_start(*halves(fold_core(act, grad_rows, down_got) if FLAGS["dfold"] else down_got))
     if FLAGS["ufold"]:
@@ -791,7 +802,7 @@
         grad_up = matmul_left_t(norm_m, grad_pre).astype(jnp.bfloat16)
         up_held = fold_part(grad_up)
         if FLAGS["upfirst"]:
-            grad_pre = after(grad_pre, grad_up)
+            grad_pre, grad_up = lax.optimization_barrier((grad_pre, grad_up))
     grad_norm_m = matmul_right_t(grad_pre, up_full)
     grad_gain_two = jnp.sum(grad_norm_m * mixed_normed, axis=0)
     grad_mixed_norm = norm_back(mixed_normed, mixed_scale, gain_two, grad_norm_m)
@@ -806,28 +817,20 @@
         "b2", grad_attn, grad_branch, down_near, up_held, home, deltas
     )
     down_line, up_near = fold_end(*down_near), fold_start(*halves(up_held))
-    if FLAGS["home"] == 2:
-        home = [swap_ctx(deltas[0], RETURN[0])]
     grad_q, grad_k, grad_v = attend_back(queries, keys, values, grad_attn, probs, starts)
-    grad_q, grad_k, grad_v, down_line, up_near, home, deltas = meet(
-        "b3", grad_q, grad_k, grad_v, down_line, up_near, home, deltas
-    )
-    if FLAGS["home"] == 2:
-        home = home + [swap_ctx(deltas[j], RETURN[j]) for j in (1, 2)]
+    grad_q, grad_k, grad_v, down_line, up_near, act = meet("b3", grad_q, grad_k, grad_v, down_line, up_near, act)
     up_line = fold_end(*up_near)
-    if FLAGS["dz"]:
-        down_pair = fold_near_z(down_line)
+    down_pair = fold_near_z(down_line)
     grad_kv = jnp.concatenate([grad_k, grad_v], axis=1)
     grad_norm_keys = matmul_right_t(grad_kv, second)
     grad_below = grad_norm_keys[: KEYS - ROWS].astype(jnp.bfloat16)
+    if FLAGS["dxfirst"]:
+        grad_kv, grad_q, grad_below = lax.optimization_barrier((grad_kv, grad_q, grad_below))
     sent = [grad_below[4 * local_len :], grad_below[local_len : 4 * local_len], grad_below[:local_len]]
-    back = []
-    for part, pairs in zip(sent, UP):
-        if FLAGS["c"] and len(back) == 2:
-            part = after(part, back)
-        back.append(swap_ctx(part, [(high, low) for low, high in pairs]))
-    if FLAGS["dxfirst"]:
-        grad_kv, grad_q = after((grad_kv, grad_q), grad_below)
+    swaps = [[(high, low) for low, high in pairs] for pairs in UP]
+    back = [swap_ctx(sent[i], swaps[i]) for i in range(2)]
+    if FLAGS["u2"] == 1:
+        grad_kv, grad_q, up_line, down_pair = lax.optimization_barrier((grad_kv, grad_q, up_line, down_pair))
     grad_norm_q = matmul_right_t(grad_q, q_full)
     grad_gain_one = jnp.sum(grad_norm_keys * key_normed, axis=0)
     grad_gain_one = grad_gain_one + jnp.sum(grad_norm_q * key_normed[KEYS - ROWS :], axis=0)
@@ -835,53 +838,69 @@
     _, core, _, _ = grid_place()
     grad_q_weight = matmul_left_t(norm_a, grad_q).astype(jnp.bfloat16)
     grad_kv_weight = matmul_left_t(norm_keys, grad_kv).astype(jnp.bfloat16)
-    if not FLAGS["outin"]:
-        grad_out = matmul_left_t(attn, grad_branch).astype(jnp.bfloat16)
     early_parts = [part.reshape(2, 2, 8 * rows_own, -1) for part in (grad_q_weight, grad_kv_weight, grad_out, gains)]
-    early_got = swap_seq(jnp.concatenate([pick(part, 1 - core, 1) for part in early_parts], axis=-1), CORE_SWAP)
+    early_sent = jnp.concatenate([pick(part, 1 - core, 1) for part in early_parts], axis=-1)
+    if FLAGS["u2"] == 2:
+        early_sent, up_line, down_pair = lax.optimization_barrier((early_sent, up_line, down_pair))
+    if FLAGS["dfar"]:
+        grad_down = fold_far_z(down_pair)
+    if FLAGS["ab"] == 1:
+        early_sent, back = meet("ab", early_sent, back)
+    early_got = swap_seq(early_sent, CORE_SWAP)
     early_held = add_low(jnp.concatenate([pick(part, core, 1) for part in early_parts], axis=-1), early_got)
-    early_held, up_line = meet("b4", early_held, up_line)
-    if FLAGS["home"] != 0:
-        home, up_line = meet("b5", home, up_line)
-        result = at_home(home, tokens, ctx)
+    if FLAGS["dfar"]:
+        if FLAGS["b4"] == 1:
+            early_held, up_line, grad_down, back = meet("b4", early_held, up_line, grad_down, back)
+        else:
+            early_held, up_line = meet("b4", early_held, up_line)
+    elif FLAGS["b4"] == 1:
+        early_held, up_line, down_pair, back = meet("b4", early_held, up_line, down_pair, back)
+    else:
+        early_held, up_line, down_pair = meet("b4", early_held, up_line, down_pair)
+    if FLAGS["late_result"]:
+        early_held, act = lax.optimization_barrier((early_held, act))
+        result_delta = (branch + matmul(act, down_full)).astype(jnp.bfloat16)
+    deltas = result_delta.reshape(3, local_len, width)
     early_held = early_held.reshape(2, 4, 2, rows_own, -1)
-    early_left, early_right = early_held[..., : 2 * width], early_held[..., 2 * width :]
-    early_near = fold_start(early_left, early_right)
-    if not FLAGS["dz"]:
-        up_line = jnp.concatenate(
-            [up_line] + [down_line[:, i * rows_own : (i + 1) * rows_own] for i in range(4)], axis=2
-        )
-    if FLAGS["lz"] == 0:
-        up_pair = fold_near_z(up_line)
-        early_near, back, up_pair = meet("b6", early_near, back, up_pair)
-    else:
-        early_near, back, up_line = meet("b6", early_near, back, up_line)
-        up_pair = fold_near_z(up_line)
+    early_near = fold_start(early_held[..., : 2 * width], early_held[..., 2 * width :])
+    last = sent[2]
+    if FLAGS["b4"] == 3:
+        early_near, back, last = meet("b4", early_near, back, last)
+    elif FLAGS["c"]:
+        back, last = meet("c", back, last)
+    back = back + [swap_ctx(last, swaps[2])]
+    if FLAGS["b6"] == 2:
+        early_near, up_line, down_pair = meet("b6", early_near, up_line, down_pair)
+    if not FLAGS["dfar"]:
+        grad_down = fold_far_z(down_pair)
+    up_pair = fold_near_z(up_line)
+    if FLAGS["b6"] == 1:
+        early_near, up_pair, grad_down, back = meet("b6", early_near, up_pair, grad_down, back)
     early_line = fold_end(*early_near)
-    early_line, up_pair = meet("b7", early_line, up_pair)
     grad_norm_a = grad_norm_keys[KEYS - ROWS :] + grad_norm_q + back[0].astype(jnp.float32) + back[1].astype(jnp.float32)
     grad_norm_a = grad_norm_a + jnp.pad(back[2].astype(jnp.float32), ((2 * local_len, 0), (0, 0)))
     grad_input_norm = norm_back(
         key_normed[KEYS - ROWS :], key_scale[KEYS - ROWS :], gain_one, grad_norm_a
     )
     grad_delta = (grad_mixed_norm + grad_input_norm).astype(jnp.bfloat16)
-    if FLAGS["ez"]:
-        early_sum = fold_far_z(fold_near_z(early_line))
-    else:
-        early_sum = fold_z(early_line)
-    if FLAGS["home"] == 0:
-        deltas = jnp.stack([deltas, grad_delta.reshape(3, local_len, width)], axis=1)
-        parts = send_home(deltas)
-        result = at_home([part[:local_len] for part in parts], tokens, ctx)
-        grad_tokens = at_home([part[local_len:] for part in parts], cotangent, ctx)
-    else:
-        grad_tokens = at_home(send_home(grad_delta), cotangent, ctx)
+    if FLAGS["lz"] == 1:
+        early_line, up_pair = meet("lz", early_line, up_pair)
     late_sum = fold_far_z(up_pair)
-    grad_up = late_sum[:, :ff]
-    if FLAGS["dz"]:
-        grad_down = fold_far_z(down_pair)
-    else:
-        grad_down = jnp.concatenate([late_sum[:, ff + i * width : ff + (i + 1) * width] for i in range(4)], axis=0)
+    deltas = jnp.stack([deltas, grad_delta.reshape(3, local_len, width)], axis=1)
+    if FLAGS["homeg"] == 1:
+        deltas, early_line = meet("homeg", deltas, early_line)
+    early_pair = fold_near_z(early_line)
+    if FLAGS["homeg"] == 2:
+        deltas, early_pair = meet("homeg", deltas, early_pair)
+    parts = send_home(deltas)
+    if FLAGS["b7"]:
+        early_pair, late_sum = meet("b7", early_pair, late_sum)
+    early_sum = fold_far_z(early_pair)
+    if FLAGS["homeg"] == 3:
+        early_sum, parts = meet("homeg", early_sum, parts)
+    result = at_home([part[:local_len] for part in parts], tokens, ctx)
+    grad_tokens = at_home([part[local_len:] for part in parts], cotangent, ctx)
+    grad_up = late_sum
     grad_qkv, grad_out = early_sum[:, : 3 * width], early_sum[:, 3 * width : 4 * width]
     grad_gain_one, grad_gain_two = early_sum[:, 4 * width], early_sum[:, 4 * width + 1]
     shape = (micro_count, 1, local_len, res_width)

time: 328 us -> 307 us (0.936)
  the two profiles are of different devices: /device:TPU:0 before, /device:TPU:5 now
where the time goes in v1:
time: 307 us; the launch traced here: 303 us
  starting transfers between devices  88.9 us (29%)
  waiting for transfers between devices  84.7 us (28%)
  Pallas kernels  32.9 us (11%)
  matrix products  31.8 us (10%)
  local copies, waits for them, and re-layouts  31.2 us (10%)
  other arithmetic  30.2 us (10%)
    ppermute x39, starting transfers between devices, swap_ctx(): return lax.ppermute(array, 'ctx', pairs)  62.1 us
    ppermute x39, waiting for transfers between devices, swap_ctx(): return lax.ppermute(array, 'ctx', pairs)  61.5 us
    ppermute x27, starting transfers between devices, swap_seq(): return lax.ppermute(array, 'seq', pairs)  26.7 us
    ppermute x27, waiting for transfers between devices, swap_seq(): return lax.ppermute(array, 'seq', pairs)  23.3 us
    pallas_call x1, Pallas kernels, attend_back(): pl.pallas_call(attend_back_kernel, grid_spec=pltpu.PrefetchScalarGridSpec...  13.4 us
    pallas_call x1, Pallas kernels, attend(): pl.pallas_call(attend_kernel, grid_spec=pltpu.PrefetchScalarGridSpec(num_...  13 us
    dot_general x5, matrix products, matmul_left_t(): lax.dot_general(left, right, (((0,), (0,)), ((), ())), preferred_element_...  12.9 us
    dot_general x5, matrix products, matmul_right_t(): lax.dot_general(left, right, (((1,), (1,)), ((), ())), preferred_element_...  11 us
  transfers between devices with their start and end apart: 66, of which 23 were waited for; matrix products, arithmetic and copies ran while one was open for 22% of the time, Pallas kernels for 11%

profile of v1, /device:TPU:5, one launch (start us, length us, event | category | flops | bytes accessed | tf_op | source)
XLA Modules:
  0.0 302.6 jit_solution(13922318806934850230)
XLA Ops:
  2.4 2.4 collective-permute-start.4
  6.6 2.6 collective-permute-start.2
  9.2 1.9 collective-permute-start
  14.7 4.8 %collective-permute-start.5 = (bf16[2,24,2432]{2,1,0:T(8,128)(2,1)S(1)}, bf16[2,24,2432]{2,1,0:T(8,128)(2,1)S(1)}, u32[]{:S(2)}, u32[]{:S(2)}) collective-permute-start(bf16[2,24,2432]{2,1,0:T(8,128)(2,1)S(1)} %get-tuple-element.276), channel_id=1, source_target_pairs={{0,2},{1,3},{2,0},{3,1},{4,6},{5,7},{6,4},{7,5},{8,10},{9,11},{10,... | collective-permute-start | bytes 700424 | tf_op jit(solution)/shard_map/ppermute | solution.py:340
  19.6 3.9 %collective-permute-done.5 = bf16[2,24,2432]{2,1,0:T(8,128)(2,1)S(1)} collective-permute-done((bf16[2,24,2432]{2,1,0:T(8,128)(2,1)S(1)}, bf16[2,24,2432]{2,1,0:T(8,128)(2,1)S(1)}, u32[]{:S(2)}, u32[]{:S(2)}) %collective-permute-start.5) | collective-permute-done | bytes 233504 | tf_op jit(solution)/shard_map/ppermute | solution.py:340
  23.6 2.5 collective-permute-start.8
  29.1 2.4 collective-permute-done.7
  32.1 3.7 %collective-permute-start.9 = (bf16[2,24,3840]{2,1,0:T(8,128)(2,1)S(1)}, bf16[2,24,3840]{2,1,0:T(8,128)(2,1)S(1)}, u32[]{:S(2)}, u32[]{:S(2)}) collective-permute-start(bf16[2,24,3840]{2,1,0:T(8,128)(2,1)S(1)} %pad_maximum_fusion.16), channel_id=1, source_target_pairs={{0,2},{1,3},{2,0},{3,1},{4,6},{5,7},{6,4},{7,5},{8,10},{9,11},{10,... | collective-permute-start | bytes 1105928 | tf_op jit(solution)/shard_map/ppermute | solution.py:340
  36.9 2.9 collective-permute-start.30
  41.1 2.0 collective-permute-done.9
  43.2 6.4 %collective-permute-done.11.refs_3_ = bf16[2,2,2,24,1152]{4,3,2,1,0:T(8,128)(2,1)} collective-permute-done((bf16[2,2,2,24,1152]{4,3,2,1,0:T(8,128)(2,1)S(1)}, bf16[2,2,2,24,1152]{4,3,2,1,0:T(8,128)(2,1)}, u32[]{:S(2)}, u32[]{:S(2)}) %collective-permute-start.11) | collective-permute-done | bytes 442400 | tf_op jit(solution)/shard_map/ppermute | solution.py:336
  50.7 3.7 %collective-permute-start.12 = (bf16[96,768]{1,0:T(8,128)(2,1)S(1)}, bf16[96,768]{1,0:T(8,128)(2,1)S(1)}, u32[]{:S(2)}, u32[]{:S(2)}) collective-permute-start(bf16[96,768]{1,0:T(8,128)(2,1)S(1)} %pad.34), channel_id=1, source_target_pairs={{0,4},{1,5},{2,6},{3,7},{4,0},{5,1},{6,2},{7,3},{8,12},{9,13},{10,... | collective-permute-start | bytes 442376 | tf_op jit(solution)/shard_map/ppermute | solution.py:340
  55.7 1.9 collective-permute-start.32
  57.6 1.9 collective-permute-start.31
  60.8 3.4 %collective-permute-start.21 = (bf16[2,2,2,24,1152]{4,3,2,1,0:T(8,128)(2,1)S(1)}, bf16[2,2,2,24,1152]{4,3,2,1,0:T(8,128)(2,1)S(1)}, u32[]{:S(2)}, u32[]{:S(2)}) collective-permute-start(bf16[2,2,2,24,1152]{4,3,2,1,0:T(8,128)(2,1)S(1)} %pad_maximum_fusion.14.refs_1_), channel_id=1, source_target_pairs={{0,8},{8,0},{16,24},{24,16},{1,9},{9,1},{17,25},{25,17},{2,10},{10... | collective-permute-start | bytes 1327112 | tf_op jit(solution)/shard_map/ppermute | solution.py:336
  64.3 2.3 collective-permute-start.13
  70.6 1.7 collective-permute-start.15
  72.3 3.1 %collective-permute-done.13 = bf16[2,96,768]{2,1,0:T(8,128)(2,1)S(1)} collective-permute-done((bf16[2,96,768]{2,1,0:T(8,128)(2,1)S(1)}, bf16[2,96,768]{2,1,0:T(8,128)(2,1)S(1)}, u32[]{:S(2)}, u32[]{:S(2)}) %collective-permute-start.13) | collective-permute-done | bytes 294944 | tf_op jit(solution)/shard_map/ppermute | solution.py:340
  79.1 3.0 collective-permute-start.18
  83.6 2.2 place.3
  85.9 1.8 copy-done.1
  88.3 10.4 %collective-permute-done.18 = bf16[288,768]{1,0:T(8,128)(2,1)} collective-permute-done((bf16[288,768]{1,0:T(8,128)(2,1)}, bf16[288,768]{1,0:T(8,128)(2,1)}, u32[]{:S(2)}, u32[]{:S(2)}) %collective-permute-start.18) | collective-permute-done | bytes 442400 | tf_op jit(solution)/shard_map/ppermute | solution.py:340
  102.2 1.8 convert_reduce_fusion
  104.1 1.8 multiply_convert_fusion.1
  105.9 2.2 fusion.60
  109.5 2.4 convolution_convert_fusion.2
  116.0 2.9 place.4
  119.0 13.0 %attend.1 = (bf16[288,768]{1,0:T(8,128)(2,1)S(1)}, bf16[3,3,768,384]{3,2,1,0:T(8,128)(2,1)S(1)}) custom-call(s32[3]{0:T(128)S(1)} %clamp_multiply_fusion.starts, bf16[288,768]{1,0:T(8,128)(2,1)S(1)} %fusion.18.q_ref, bf16[960,768]{1,0:T(8,128)(2,1)S(1)} %get-tuple-element.124.k_ref, bf16[960,768]{1,0:T(8,128)(2,1)S(1)} %get-tuple-element.125.v_ref, ...), custom_call_target="tpu_custom_call" | custom-call | flops 3000000000 | bytes 12000000 | tf_op jit(solution)/shard_map/attend/pallas_call | solution.py:551
  132.0 1.8 fusion.61
  134.5 1.6 fusion.4
  139.1 3.1 %convolution_convert_fusion.1 = bf16[3072,768]{1,0:T(8,128)(2,1)S(1)} fusion(bf16[288,3072]{1,0:T(8,128)(2,1)S(1)} %multiply_convert_fusion, bf16[288,768]{1,0:T(8,128)(2,1)S(1)} %copy-done.46), kind=kOutput, calls=%fused_computation.3 | convolution fusion | flops 1361313792 | bytes 6930432 | tf_op jit(solution)/shard_map/dot_general | solution.py:36
  142.2 1.8 constant_dynamic-slice_fusion.5
  144.0 1.5 copy.72
  151.5 3.4 %fusion.12 = bf16[288,3072]{1,0:T(8,128)(2,1)S(1)} fusion(f32[288,3072]{1,0:T(8,128)S(1)} %copy-done.35, bf16[288,768]{1,0:T(8,128)(2,1)S(1)} %copy-done.46, bf16[3072,768]{1,0:T(8,128)(2,1)S(1)} %bitcast.263), kind=kOutput, calls=%fused_computation.20 | convolution fusion | flops 1376649216 | bytes 10469376 | tf_op jit(solution)/shard_map/dot_general | solution.py:42
  154.9 2.4 fusion.1
  158.5 3.2 %convolution_convert_fusion = bf16[768,3072]{1,0:T(8,128)(2,1)S(1)} fusion(bf16[288,3072]{1,0:T(8,128)(2,1)S(1)} %fusion.12, f32[288,768]{1,0:T(8,128)S(1)} %copy-done.32, f32[768]{0:T(1024)S(1)} %copy-done.62, f32[288]{0:T(512)S(1)} %copy-done.68, f32[288]{0:T(512)S(1)} %copy-done.66, pred[768]{0:T(1024)(128)(4,1)S(1)} %copy-done.55), kind=kOutput, calls=%fused_computation.2 | convolution fusion | flops 1362198528 | bytes 7378944 | tf_op jit(solution)/shard_map/dot_general | solution.py:36
  163.1 1.7 multiply_reduce_fusion.3
  166.1 1.8 convolution_convert_fusion.4
  168.0 4.5 %collective-permute-done.40 = bf16[4,2,96,384]{3,2,0,1:T(8,128)(2,1)S(1)} collective-permute-done((bf16[4,2,96,384]{3,2,0,1:T(8,128)(2,1)S(1)}, bf16[4,2,96,384]{3,2,0,1:T(8,128)(2,1)S(1)}, u32[]{:S(2)}, u32[]{:S(2)}) %collective-permute-start.40) | collective-permute-done | bytes 589856 | tf_op jit(solution)/shard_map/ppermute | solution.py:336
  177.3 13.4 %attend_back.1 = (bf16[288,768]{1,0:T(8,128)(2,1)S(1)}, bf16[960,768]{1,0:T(8,128)(2,1)S(1)}, bf16[960,768]{1,0:T(8,128)(2,1)S(1)}) custom-call(s32[3]{0:T(128)S(1)} %clamp_multiply_fusion.starts, bf16[288,768]{1,0:T(8,128)(2,1)S(1)} %copy-done.25, bf16[960,768]{1,0:T(8,128)(2,1)S(1)} %copy-done.8, bf16[960,768]{1,0:T(8,128)(2,1)S(1)} %copy-done.6, ...), custom_call_target="tpu_custom_call" | custom-call | flops 7000000000 | bytes 14000000 | tf_op jit(solution)/shard_map/attend_back/pallas_call | solution.py:607
  191.0 2.8 collective-permute-done.45
  198.0 3.8 %multiply_reduce_fusion = (f32[768]{0:T(1024)S(1)}, f32[960,768]{1,0:T(8,128)S(1)}, f32[960,768]{1,0:T(8,128)S(1)}) fusion(f32[960]{0:T(1024)S(1)} %copy-done.58, f32[960]{0:T(1024)S(1)} %copy-done.64, pred[768]{0:T(1024)(128)(4,1)S(1)} %copy-done.55, bf16[288,768]{1,0:T(8,128)(2,1)} %pad_maximum_fusion.15, bf16[288,768]{1,0:T(8,128)(2,1)} %collective-permute-done.18, ...), kind=kOutput, calls=%fused_computation.23 | convolution fusion | flops 2273770752 | bytes 12693504 | tf_op jit(solution)/shard_map/dot_general | solution.py:42
  204.4 2.6 collective-permute-start.50
  208.2 1.8 convolution_convert_fusion.5
  211.5 2.9 convolution_convert_fusion.3
  217.1 2.8 dynamic-slice_bitcast_fusion.5
  219.9 1.7 pad_maximum_fusion
  221.6 2.5 collective-permute-done.50
  224.0 3.8 %collective-permute-start.52 = (bf16[2,192,3200]{2,1,0:T(8,128)(2,1)}, bf16[2,192,3200]{2,1,0:T(8,128)(2,1)}, u32[]{:S(2)}, u32[]{:S(2)}) collective-permute-start(bf16[2,192,3200]{2,1,0:T(8,128)(2,1)} %pad_maximum_fusion), channel_id=1, source_target_pairs={{0,8},{8,0},{16,24},{24,16},{1,9},{9,1},{17,25},{25,17},{2,10},{10... | collective-permute-start | bytes 7372808 | tf_op jit(solution)/shard_map/ppermute | solution.py:336
  229.5 3.0 collective-permute-done.52
  232.5 2.6 add_convert_fusion
  236.7 1.8 collective-permute-start.55
  240.2 1.6 fusion.17
  241.8 2.7 collective-permute-done.56
  245.3 2.9 collective-permute-done.55
  248.3 4.3 %collective-permute-done.53 = bf16[4,2,24,1536]{3,2,0,1:T(8,128)(2,1)S(1)} collective-permute-done((bf16[4,2,24,1536]{3,2,0,1:T(8,128)(2,1)S(1)}, bf16[4,2,24,1536]{3,2,0,1:T(8,128)(2,1)S(1)}, u32[]{:S(2)}, u32[]{:S(2)}) %collective-permute-start.53) | collective-permute-done | bytes 589856 | tf_op jit(solution)/shard_map/ppermute | solution.py:336
  252.8 1.8 collective-permute-done.54
  254.8 1.8 multiply_reduce_fusion.2
  259.4 4.3 %collective-permute-done.58 = bf16[4,24,1536]{2,1,0:T(8,128)(2,1)S(1)} collective-permute-done((bf16[4,24,1536]{2,1,0:T(8,128)(2,1)S(1)}, bf16[4,24,1536]{2,1,0:T(8,128)(2,1)S(1)}, u32[]{:S(2)}, u32[]{:S(2)}) %collective-permute-start.58) | collective-permute-done | bytes 294944 | tf_op jit(solution)/shard_map/ppermute | solution.py:340
  266.5 4.3 %collective-permute-done.60 = bf16[2,24,3200]{2,1,0:T(8,128)(2,1)S(1)} collective-permute-done((bf16[2,24,3200]{2,1,0:T(8,128)(2,1)S(1)}, bf16[2,24,3200]{2,1,0:T(8,128)(2,1)S(1)}, u32[]{:S(2)}, u32[]{:S(2)}) %collective-permute-start.60) | collective-permute-done | bytes 307232 | tf_op jit(solution)/shard_map/ppermute | solution.py:340
  272.1 1.7 collective-permute-start.62
  273.8 3.5 %collective-permute-start.63 = (bf16[192,768]{1,0:T(8,128)(2,1)S(1)}, bf16[192,768]{1,0:T(8,128)(2,1)S(1)}, u32[]{:S(2)}, u32[]{:S(2)}) collective-permute-start(bf16[192,768]{1,0:T(8,128)(2,1)S(1)} %bitcast.295), channel_id=1, source_target_pairs={{0,2},{1,5},{2,0},{3,3},{4,6},{5,1},{6,4},{7,7},{8,10},{9,13},{10,... | collective-permute-start | bytes 884744 | tf_op jit(solution)/shard_map/ppermute | solution.py:340
  277.4 1.9 collective-permute-start.61
  281.4 18.7 %collective-permute-done.61 = bf16[192,768]{1,0:T(8,128)(2,1)S(1)} collective-permute-done((bf16[192,768]{1,0:T(8,128)(2,1)S(1)}, bf16[192,768]{1,0:T(8,128)(2,1)S(1)}, u32[]{:S(2)}, u32[]{:S(2)}) %collective-permute-start.61) | collective-permute-done | bytes 294944 | tf_op jit(solution)/shard_map/ppermute | solution.py:340
  (387 shorter events, 82.5 us)
Async XLA Ops:
  2.4 12.3 %collective-permute-start.4 = (bf16[24,2432]{1,0:T(8,128)(2,1)S(1)}, bf16[24,2432]{1,0:T(8,128)(2,1)S(1)}, u32[]{:S(2)}, u32[]{:S(2)}) collective-permute-start(bf16[24,2432]{1,0:T(8,128)(2,1)S(1)} %get-tuple-element.280), channel_id=1, source_target_pairs={{0,4},{1,5},{2,6},{3,7},{4,0},{5,1},{6,2},{7,3},{8,12},{9,13},{10,... | collective-permute-start | bytes 350216 | tf_op jit(solution)/shard_map/ppermute | solution.py:340
  5.9 17.6 %collective-permute-start.3 = (bf16[96,768]{1,0:T(8,128)(2,1)S(1)}, bf16[96,768]{1,0:T(8,128)(2,1)S(1)}, u32[]{:S(2)}, u32[]{:S(2)}) collective-permute-start(bf16[96,768]{1,0:T(8,128)(2,1)S(1)} %get-tuple-element.265), channel_id=1, source_target_pairs={{0,5},{8,13},{16,21},{24,29}} | collective-permute-start | bytes 442376 | tf_op jit(solution)/shard_map/ppermute | solution.py:340
  6.6 16.9 %collective-permute-start.2 = (bf16[96,768]{1,0:T(8,128)(2,1)S(1)}, bf16[96,768]{1,0:T(8,128)(2,1)S(1)}, u32[]{:S(2)}, u32[]{:S(2)}) collective-permute-start(bf16[96,768]{1,0:T(8,128)(2,1)S(1)} %get-tuple-element.266), channel_id=1, source_target_pairs={{2,0},{5,1},{0,2},{3,3},{6,4},{1,5},{4,6},{7,7},{10,8},{13,9},{8,1... | collective-permute-start | bytes 442376 | tf_op jit(solution)/shard_map/ppermute | solution.py:340
  9.2 14.3 %collective-permute-start = (bf16[96,768]{1,0:T(8,128)(2,1)S(1)}, bf16[96,768]{1,0:T(8,128)(2,1)S(1)}, u32[]{:S(2)}, u32[]{:S(2)}) collective-permute-start(bf16[96,768]{1,0:T(8,128)(2,1)S(1)} %get-tuple-element.267), channel_id=1, source_target_pairs={{0,0},{3,1},{6,2},{1,3},{4,4},{7,5},{2,6},{5,7},{8,8},{11,9},{14,1... | collective-permute-start | bytes 442376 | tf_op jit(solution)/shard_map/ppermute | solution.py:340
  11.2 12.4 %collective-permute-start.1 = (bf16[96,768]{1,0:T(8,128)(2,1)S(1)}, bf16[96,768]{1,0:T(8,128)(2,1)S(1)}, u32[]{:S(2)}, u32[]{:S(2)}) collective-permute-start(bf16[96,768]{1,0:T(8,128)(2,1)S(1)} %get-tuple-element.268), channel_id=1, source_target_pairs={{1,0},{4,1},{7,2},{2,3},{5,4},{0,5},{3,6},{6,7},{9,8},{12,9},{15,1... | collective-permute-start | bytes 442376 | tf_op jit(solution)/shard_map/ppermute | solution.py:340
  14.7 8.8 %collective-permute-start.5 = (bf16[2,24,2432]{2,1,0:T(8,128)(2,1)S(1)}, bf16[2,24,2432]{2,1,0:T(8,128)(2,1)S(1)}, u32[]{:S(2)}, u32[]{:S(2)}) collective-permute-start(bf16[2,24,2432]{2,1,0:T(8,128)(2,1)S(1)} %get-tuple-element.276), channel_id=1, source_target_pairs={{0,2},{1,3},{2,0},{3,1},{4,6},{5,7},{6,4},{7,5},{8,10},{9,11},{10,... | collective-permute-start | bytes 700424 | tf_op jit(solution)/shard_map/ppermute | solution.py:340
  23.6 5.4 %collective-permute-start.8 = (bf16[24,3840]{1,0:T(8,128)(2,1)S(1)}, bf16[24,3840]{1,0:T(8,128)(2,1)S(1)}, u32[]{:S(2)}, u32[]{:S(2)}) collective-permute-start(bf16[24,3840]{1,0:T(8,128)(2,1)S(1)} %fusion.45), channel_id=1, source_target_pairs={{0,4},{1,5},{2,6},{3,7},{4,0},{5,1},{6,2},{7,3},{8,12},{9,13},{10,... | collective-permute-start | bytes 552968 | tf_op jit(solution)/shard_map/ppermute | solution.py:340
  26.2 5.3 %collective-permute-start.7 = (bf16[2,2,24,1152]{3,2,1,0:T(8,128)(2,1)S(1)}, bf16[2,2,24,1152]{3,2,1,0:T(8,128)(2,1)S(1)}, u32[]{:S(2)}, u32[]{:S(2)}) collective-permute-start(bf16[2,2,24,1152]{3,2,1,0:T(8,128)(2,1)S(1)} %get-tuple-element.259), channel_id=1, source_target_pairs={{0,1},{1,0},{2,3},{3,2},{4,5},{5,4},{6,7},{7,6},{8,9},{9,8},{10,11... | collective-permute-start | bytes 663560 | tf_op jit(solution)/shard_map/ppermute | solution.py:340
  26.2 5.8 %collective-permute-start.6 = (bf16[2,2,24,1280]{3,2,1,0:T(8,128)(2,1)S(1)}, bf16[2,2,24,1280]{3,2,1,0:T(8,128)(2,1)S(1)}, u32[]{:S(2)}, u32[]{:S(2)}) collective-permute-start(bf16[2,2,24,1280]{3,2,1,0:T(8,128)(2,1)S(1)} %get-tuple-element.261), channel_id=1, source_target_pairs={{0,16},{8,24},{16,0},{24,8},{1,17},{9,25},{17,1},{25,9},{2,18},{10... | collective-permute-start | bytes 737288 | tf_op jit(solution)/shard_map/ppermute | solution.py:336
  32.1 11.0 %collective-permute-start.9 = (bf16[2,24,3840]{2,1,0:T(8,128)(2,1)S(1)}, bf16[2,24,3840]{2,1,0:T(8,128)(2,1)S(1)}, u32[]{:S(2)}, u32[]{:S(2)}) collective-permute-start(bf16[2,24,3840]{2,1,0:T(8,128)(2,1)S(1)} %pad_maximum_fusion.16), channel_id=1, source_target_pairs={{0,2},{1,3},{2,0},{3,1},{4,6},{5,7},{6,4},{7,5},{8,10},{9,11},{10,... | collective-permute-start | bytes 1105928 | tf_op jit(solution)/shard_map/ppermute | solution.py:340
  36.1 13.5 %collective-permute-start.10 = (bf16[2,2,2,24,1280]{4,3,2,1,0:T(8,128)(2,1)S(1)}, bf16[2,2,2,24,1280]{4,3,2,1,0:T(8,128)(2,1)}, u32[]{:S(2)}, u32[]{:S(2)}) collective-permute-start(bf16[2,2,2,24,1280]{4,3,2,1,0:T(8,128)(2,1)S(1)} %pad_maximum_fusion.12.refs_0_), channel_id=1, source_target_pairs={{0,1},{1,0},{2,3},{3,2},{4,5},{5,4},{6,7},{7,6},{8,9},{9,8},{10,11... | collective-permute-start | bytes 1474568 | tf_op jit(solution)/shard_map/ppermute | solution.py:340
  36.9 22.6 %collective-permute-start.30 = (bf16[96,768]{1,0:T(8,128)(2,1)}, bf16[96,768]{1,0:T(8,128)(2,1)S(1)}, u32[]{:S(2)}, u32[]{:S(2)}) collective-permute-start(bf16[96,768]{1,0:T(8,128)(2,1)} %get-tuple-element.264), channel_id=1, source_target_pairs={{0,0},{3,1},{6,2},{1,3},{4,4},{7,5},{2,6},{5,7},{8,8},{11,9},{14,1... | collective-permute-start | bytes 442376 | tf_op jit(solution)/shard_map/ppermute | solution.py:340
  39.8 9.8 %collective-permute-start.11 = (bf16[2,2,2,24,1152]{4,3,2,1,0:T(8,128)(2,1)S(1)}, bf16[2,2,2,24,1152]{4,3,2,1,0:T(8,128)(2,1)}, u32[]{:S(2)}, u32[]{:S(2)}) collective-permute-start(bf16[2,2,2,24,1152]{4,3,2,1,0:T(8,128)(2,1)S(1)} %pad_maximum_fusion.14.refs_1_), channel_id=1, source_target_pairs={{0,16},{8,24},{16,0},{24,8},{1,17},{9,25},{17,1},{25,9},{2,18},{10... | collective-permute-start | bytes 1327112 | tf_op jit(solution)/shard_map/ppermute | solution.py:336
  49.7 14.6 %collective-permute-start.16 = (bf16[2,2,24,1920]{3,2,1,0:T(8,128)(2,1)S(1)}, bf16[2,2,24,1920]{3,2,1,0:T(8,128)(2,1)S(1)}, u32[]{:S(2)}, u32[]{:S(2)}) collective-permute-start(bf16[2,2,24,1920]{3,2,1,0:T(8,128)(2,1)S(1)} %get-tuple-element.252), channel_id=1, source_target_pairs={{0,1},{1,0},{2,3},{3,2},{4,5},{5,4},{6,7},{7,6},{8,9},{9,8},{10,11... | collective-permute-start | bytes 1105928 | tf_op jit(solution)/shard_map/ppermute | solution.py:340
  50.7 10.1 %collective-permute-start.12 = (bf16[96,768]{1,0:T(8,128)(2,1)S(1)}, bf16[96,768]{1,0:T(8,128)(2,1)S(1)}, u32[]{:S(2)}, u32[]{:S(2)}) collective-permute-start(bf16[96,768]{1,0:T(8,128)(2,1)S(1)} %pad.34), channel_id=1, source_target_pairs={{0,4},{1,5},{2,6},{3,7},{4,0},{5,1},{6,2},{7,3},{8,12},{9,13},{10,... | collective-permute-start | bytes 442376 | tf_op jit(solution)/shard_map/ppermute | solution.py:340
  55.7 13.1 %collective-permute-start.32 = (bf16[96,768]{1,0:T(8,128)(2,1)}, bf16[96,768]{1,0:T(8,128)(2,1)S(1)}, u32[]{:S(2)}, u32[]{:S(2)}) collective-permute-start(bf16[96,768]{1,0:T(8,128)(2,1)} %get-tuple-element.262), channel_id=1, source_target_pairs={{2,0},{5,1},{0,2},{3,3},{6,4},{1,5},{4,6},{7,7},{10,8},{13,9},{8,1... | collective-permute-start | bytes 442376 | tf_op jit(solution)/shard_map/ppermute | solution.py:340
  57.6 12.1 %collective-permute-start.31 = (bf16[96,768]{1,0:T(8,128)(2,1)}, bf16[96,768]{1,0:T(8,128)(2,1)S(1)}, u32[]{:S(2)}, u32[]{:S(2)}) collective-permute-start(bf16[96,768]{1,0:T(8,128)(2,1)} %get-tuple-element.263), channel_id=1, source_target_pairs={{1,0},{4,1},{7,2},{2,3},{5,4},{0,5},{3,6},{6,7},{9,8},{12,9},{15,1... | collective-permute-start | bytes 442376 | tf_op jit(solution)/shard_map/ppermute | solution.py:340
  59.5 10.2 %collective-permute-start.14 = (bf16[2,2,24,1920]{3,2,1,0:T(8,128)(2,1)S(1)}, bf16[2,2,24,1920]{3,2,1,0:T(8,128)(2,1)S(1)}, u32[]{:S(2)}, u32[]{:S(2)}) collective-permute-start(bf16[2,2,24,1920]{3,2,1,0:T(8,128)(2,1)S(1)} %get-tuple-element.253), channel_id=1, source_target_pairs={{0,16},{8,24},{16,0},{24,8},{1,17},{9,25},{17,1},{25,9},{2,18},{10... | collective-permute-start | bytes 1105928 | tf_op jit(solution)/shard_map/ppermute | solution.py:336
  60.8 9.9 %collective-permute-start.21 = (bf16[2,2,2,24,1152]{4,3,2,1,0:T(8,128)(2,1)S(1)}, bf16[2,2,2,24,1152]{4,3,2,1,0:T(8,128)(2,1)S(1)}, u32[]{:S(2)}, u32[]{:S(2)}) collective-permute-start(bf16[2,2,2,24,1152]{4,3,2,1,0:T(8,128)(2,1)S(1)} %pad_maximum_fusion.14.refs_1_), channel_id=1, source_target_pairs={{0,8},{8,0},{16,24},{24,16},{1,9},{9,1},{17,25},{25,17},{2,10},{10... | collective-permute-start | bytes 1327112 | tf_op jit(solution)/shard_map/ppermute | solution.py:336
  64.3 11.2 %collective-permute-start.13 = (bf16[2,96,768]{2,1,0:T(8,128)(2,1)S(1)}, bf16[2,96,768]{2,1,0:T(8,128)(2,1)S(1)}, u32[]{:S(2)}, u32[]{:S(2)}) collective-permute-start(bf16[2,96,768]{2,1,0:T(8,128)(2,1)S(1)} %get-tuple-element.274), channel_id=1, source_target_pairs={{0,2},{1,3},{2,0},{3,1},{4,6},{5,7},{6,4},{7,5},{8,10},{9,11},{10,... | collective-permute-start | bytes 884744 | tf_op jit(solution)/shard_map/ppermute | solution.py:340
  68.8 8.9 %collective-permute-start.20 = (bf16[2,2,2,24,1280]{4,3,2,1,0:T(8,128)(2,1)S(1)}, bf16[2,2,2,24,1280]{4,3,2,1,0:T(8,128)(2,1)S(1)}, u32[]{:S(2)}, u32[]{:S(2)}) collective-permute-start(bf16[2,2,2,24,1280]{4,3,2,1,0:T(8,128)(2,1)S(1)} %pad_maximum_fusion.12.refs_0_), channel_id=1, source_target_pairs={{0,8},{8,0},{16,24},{24,16},{1,9},{9,1},{17,25},{25,17},{2,10},{10... | collective-permute-start | bytes 1474568 | tf_op jit(solution)/shard_map/ppermute | solution.py:336
  69.7 9.4 %collective-permute-start.23 = (bf16[2,2,2,24,1152]{4,3,2,1,0:T(8,128)(2,1)}, bf16[2,2,2,24,1152]{4,3,2,1,0:T(8,128)(2,1)S(1)}, u32[]{:S(2)}, u32[]{:S(2)}) collective-permute-start(bf16[2,2,2,24,1152]{4,3,2,1,0:T(8,128)(2,1)} %collective-permute-done.11.refs_3_), channel_id=1, source_target_pairs={{0,8},{8,0},{16,24},{24,16},{1,9},{9,1},{17,25},{25,17},{2,10},{10... | collective-permute-start | bytes 1327112 | tf_op jit(solution)/shard_map/ppermute | solution.py:336
  69.7 12.4 %collective-permute-start.22 = (bf16[2,2,2,24,1280]{4,3,2,1,0:T(8,128)(2,1)}, bf16[2,2,2,24,1280]{4,3,2,1,0:T(8,128)(2,1)S(1)}, u32[]{:S(2)}, u32[]{:S(2)}) collective-permute-start(bf16[2,2,2,24,1280]{4,3,2,1,0:T(8,128)(2,1)} %collective-permute-done.10.refs_2_), channel_id=1, source_target_pairs={{0,8},{8,0},{16,24},{24,16},{1,9},{9,1},{17,25},{25,17},{2,10},{10... | collective-permute-start | bytes 1474568 | tf_op jit(solution)/shard_map/ppermute | solution.py:336
  70.6 28.1 %collective-permute-start.15 = (bf16[2,2,2,24,1920]{4,3,2,1,0:T(8,128)(2,1)S(1)}, bf16[2,2,2,24,1920]{4,3,2,1,0:T(8,128)(2,1)S(1)}, u32[]{:S(2)}, u32[]{:S(2)}) collective-permute-start(bf16[2,2,2,24,1920]{4,3,2,1,0:T(8,128)(2,1)S(1)} %pad_maximum_fusion.4.refs_0_), channel_id=1, source_target_pairs={{0,1},{1,0},{2,3},{3,2},{4,5},{5,4},{6,7},{7,6},{8,9},{9,8},{10,11... | collective-permute-start | bytes 2211848 | tf_op jit(solution)/shard_map/ppermute | solution.py:340
  75.5 23.2 %collective-permute-start.17 = (bf16[2,2,2,24,1920]{4,3,2,1,0:T(8,128)(2,1)S(1)}, bf16[2,2,2,24,1920]{4,3,2,1,0:T(8,128)(2,1)}, u32[]{:S(2)}, u32[]{:S(2)}) collective-permute-start(bf16[2,2,2,24,1920]{4,3,2,1,0:T(8,128)(2,1)S(1)} %pad_maximum_fusion.5.refs_1_), channel_id=1, source_target_pairs={{0,16},{8,24},{16,0},{24,8},{1,17},{9,25},{17,1},{25,9},{2,18},{10... | collective-permute-start | bytes 2211848 | tf_op jit(solution)/shard_map/ppermute | solution.py:336
  77.7 10.5 %collective-permute-start.19 = (bf16[288,768]{1,0:T(8,128)(2,1)}, bf16[288,768]{1,0:T(8,128)(2,1)}, u32[]{:S(2)}, u32[]{:S(2)}) collective-permute-start(bf16[288,768]{1,0:T(8,128)(2,1)} %pad_maximum_fusion.15), channel_id=1, source_target_pairs={{0,2},{2,4},{3,5},{5,7},{8,10},{10,12},{11,13},{13,15},{16,18},{18... | collective-permute-start | bytes 1327112 | tf_op jit(solution)/shard_map/ppermute | solution.py:340
  79.1 19.6 %collective-permute-start.18 = (bf16[288,768]{1,0:T(8,128)(2,1)}, bf16[288,768]{1,0:T(8,128)(2,1)}, u32[]{:S(2)}, u32[]{:S(2)}) collective-permute-start(bf16[288,768]{1,0:T(8,128)(2,1)} %pad_maximum_fusion.15), channel_id=1, source_target_pairs={{0,1},{1,2},{2,3},{3,4},{4,5},{5,6},{6,7},{8,9},{9,10},{10,11},{11... | collective-permute-start | bytes 1327112 | tf_op jit(solution)/shard_map/ppermute | solution.py:340
  82.2 30.6 %collective-permute-start.26 = (bf16[2,2,2,24,1920]{4,3,2,1,0:T(8,128)(2,1)S(1)}, bf16[2,2,2,24,1920]{4,3,2,1,0:T(8,128)(2,1)}, u32[]{:S(2)}, u32[]{:S(2)}) collective-permute-start(bf16[2,2,2,24,1920]{4,3,2,1,0:T(8,128)(2,1)S(1)} %pad_maximum_fusion.4.refs_0_), channel_id=1, source_target_pairs={{0,8},{8,0},{16,24},{24,16},{1,9},{9,1},{17,25},{25,17},{2,10},{10... | collective-permute-start | bytes 2211848 | tf_op jit(solution)/shard_map/ppermute | solution.py:336
  88.2 24.6 %collective-permute-start.27 = (bf16[2,2,2,24,1920]{4,3,2,1,0:T(8,128)(2,1)S(1)}, bf16[2,2,2,24,1920]{4,3,2,1,0:T(8,128)(2,1)S(1)}, u32[]{:S(2)}, u32[]{:S(2)}) collective-permute-start(bf16[2,2,2,24,1920]{4,3,2,1,0:T(8,128)(2,1)S(1)} %pad_maximum_fusion.5.refs_1_), channel_id=1, source_target_pairs={{0,8},{8,0},{16,24},{24,16},{1,9},{9,1},{17,25},{25,17},{2,10},{10... | collective-permute-start | bytes 2211848 | tf_op jit(solution)/shard_map/ppermute | solution.py:336
  99.9 8.3 %collective-permute-start.25 = (bf16[2,2,96,384]{3,2,1,0:T(8,128)(2,1)S(1)}, bf16[2,2,96,384]{3,2,1,0:T(8,128)(2,1)S(1)}, u32[]{:S(2)}, u32[]{:S(2)}) collective-permute-start(bf16[2,2,96,384]{3,2,1,0:T(8,128)(2,1)S(1)} %get-tuple-element.256), channel_id=1, source_target_pairs={{0,1},{1,0},{2,3},{3,2},{4,5},{5,4},{6,7},{7,6},{8,9},{9,8},{10,11... | collective-permute-start | bytes 884744 | tf_op jit(solution)/shard_map/ppermute | solution.py:340
  100.0 9.5 %collective-permute-start.24 = (bf16[2,2,96,384]{3,2,1,0:T(8,128)(2,1)S(1)}, bf16[2,2,96,384]{3,2,1,0:T(8,128)(2,1)S(1)}, u32[]{:S(2)}, u32[]{:S(2)}) collective-permute-start(bf16[2,2,96,384]{3,2,1,0:T(8,128)(2,1)S(1)} %get-tuple-element.257), channel_id=1, source_target_pairs={{0,16},{8,24},{16,0},{24,8},{1,17},{9,25},{17,1},{25,9},{2,18},{10... | collective-permute-start | bytes 884744 | tf_op jit(solution)/shard_map/ppermute | solution.py:336
  101.2 11.6 %collective-permute-start.28 = (bf16[2,2,2,24,1920]{4,3,2,1,0:T(8,128)(2,1)S(1)}, bf16[2,2,2,24,1920]{4,3,2,1,0:T(8,128)(2,1)S(1)}, u32[]{:S(2)}, u32[]{:S(2)}) collective-permute-start(bf16[2,2,2,24,1920]{4,3,2,1,0:T(8,128)(2,1)S(1)} %collective-permute-done.15.refs_2_), channel_id=1, source_target_pairs={{0,8},{8,0},{16,24},{24,16},{1,9},{9,1},{17,25},{25,17},{2,10},{10... | collective-permute-start | bytes 2211848 | tf_op jit(solution)/shard_map/ppermute | solution.py:336
  108.1 4.7 %collective-permute-start.29 = (bf16[2,2,2,24,1920]{4,3,2,1,0:T(8,128)(2,1)}, bf16[2,2,2,24,1920]{4,3,2,1,0:T(8,128)(2,1)S(1)}, u32[]{:S(2)}, u32[]{:S(2)}) collective-permute-start(bf16[2,2,2,24,1920]{4,3,2,1,0:T(8,128)(2,1)} %collective-permute-done.17.refs_3_), channel_id=1, source_target_pairs={{0,8},{8,0},{16,24},{24,16},{1,9},{9,1},{17,25},{25,17},{2,10},{10... | collective-permute-start | bytes 2211848 | tf_op jit(solution)/shard_map/ppermute | solution.py:336
  112.8 21.1 %collective-permute-start.35 = (bf16[2,2,2,96,384]{4,3,2,1,0:T(8,128)(2,1)S(1)}, bf16[2,2,2,96,384]{4,3,2,1,0:T(8,128)(2,1)S(1)}, u32[]{:S(2)}, u32[]{:S(2)}) collective-permute-start(bf16[2,2,2,96,384]{4,3,2,1,0:T(8,128)(2,1)S(1)} %pad_maximum_fusion.8.refs_0_), channel_id=1, source_target_pairs={{0,1},{1,0},{2,3},{3,2},{4,5},{5,4},{6,7},{7,6},{8,9},{9,8},{10,11... | collective-permute-start | bytes 1769480 | tf_op jit(solution)/shard_map/ppermute | solution.py:340
  114.0 22.2 %collective-permute-start.33 = (bf16[2,2,2,96,384]{4,3,2,1,0:T(8,128)(2,1)S(1)}, bf16[2,2,2,96,384]{4,3,2,1,0:T(8,128)(2,1)S(1)}, u32[]{:S(2)}, u32[]{:S(2)}) collective-permute-start(bf16[2,2,2,96,384]{4,3,2,1,0:T(8,128)(2,1)S(1)} %pad_maximum_fusion.8.refs_0_), channel_id=1, source_target_pairs={{0,8},{8,0},{16,24},{24,16},{1,9},{9,1},{17,25},{25,17},{2,10},{10... | collective-permute-start | bytes 1769480 | tf_op jit(solution)/shard_map/ppermute | solution.py:336
  114.5 19.6 %collective-permute-start.37 = (bf16[2,2,2,96,384]{4,3,2,1,0:T(8,128)(2,1)S(1)}, bf16[2,2,2,96,384]{4,3,2,1,0:T(8,128)(2,1)S(1)}, u32[]{:S(2)}, u32[]{:S(2)}) collective-permute-start(bf16[2,2,2,96,384]{4,3,2,1,0:T(8,128)(2,1)S(1)} %pad_maximum_fusion.9.refs_1_), channel_id=1, source_target_pairs={{0,16},{8,24},{16,0},{24,8},{1,17},{9,25},{17,1},{25,9},{2,18},{10... | collective-permute-start | bytes 1769480 | tf_op jit(solution)/shard_map/ppermute | solution.py:336
  115.8 20.5 %collective-permute-start.34 = (bf16[2,2,2,96,384]{4,3,2,1,0:T(8,128)(2,1)S(1)}, bf16[2,2,2,96,384]{4,3,2,1,0:T(8,128)(2,1)S(1)}, u32[]{:S(2)}, u32[]{:S(2)}) collective-permute-start(bf16[2,2,2,96,384]{4,3,2,1,0:T(8,128)(2,1)S(1)} %pad_maximum_fusion.9.refs_1_), channel_id=1, source_target_pairs={{0,8},{8,0},{16,24},{24,16},{1,9},{9,1},{17,25},{25,17},{2,10},{10... | collective-permute-start | bytes 1769480 | tf_op jit(solution)/shard_map/ppermute | solution.py:336
  145.6 9.3 %collective-permute-start.39 = (bf16[2,4,2,96,768]{4,3,1,0,2:T(8,128)(2,1)}, bf16[2,4,2,96,768]{4,3,1,0,2:T(8,128)(2,1)}, u32[]{:S(2)}, u32[]{:S(2)}) collective-permute-start(bf16[2,4,2,96,768]{4,3,1,0,2:T(8,128)(2,1)} %bitcast.249), channel_id=1, source_target_pairs={{0,8},{8,0},{16,24},{24,16},{1,9},{9,1},{17,25},{25,17},{2,10},{10... | collective-permute-start | bytes 7077896 | tf_op jit(solution)/shard_map/ppermute | solution.py:336
  157.7 14.8 %collective-permute-start.40 = (bf16[4,2,96,384]{3,2,0,1:T(8,128)(2,1)S(1)}, bf16[4,2,96,384]{3,2,0,1:T(8,128)(2,1)S(1)}, u32[]{:S(2)}, u32[]{:S(2)}) collective-permute-start(bf16[4,2,96,384]{3,2,0,1:T(8,128)(2,1)S(1)} %dynamic-slice_bitcast_fusion.10), channel_id=1, source_target_pairs={{0,16},{8,24},{16,0},{24,8},{1,17},{9,25},{17,1},{25,9},{2,18},{10... | collective-permute-start | bytes 1769480 | tf_op jit(solution)/shard_map/ppermute | solution.py:336
  158.1 14.6 %collective-permute-start.41 = (bf16[2,4,96,384]{3,2,1,0:T(8,128)(2,1)S(1)}, bf16[2,4,96,384]{3,2,1,0:T(8,128)(2,1)S(1)}, u32[]{:S(2)}, u32[]{:S(2)}) collective-permute-start(bf16[2,4,96,384]{3,2,1,0:T(8,128)(2,1)S(1)} %dynamic-slice_bitcast_fusion.9), channel_id=1, source_target_pairs={{0,1},{1,0},{2,3},{3,2},{4,5},{5,4},{6,7},{7,6},{8,9},{9,8},{10,11... | collective-permute-start | bytes 1769480 | tf_op jit(solution)/shard_map/ppermute | solution.py:340
  162.2 10.6 %collective-permute-start.42 = (bf16[2,4,2,24,3072]{4,3,1,0,2:T(8,128)(2,1)S(1)}, bf16[2,4,2,24,3072]{4,3,1,0,2:T(8,128)(2,1)S(1)}, u32[]{:S(2)}, u32[]{:S(2)}) collective-permute-start(bf16[2,4,2,24,3072]{4,3,1,0,2:T(8,128)(2,1)S(1)} %bitcast.276), channel_id=1, source_target_pairs={{0,8},{8,0},{16,24},{24,16},{1,9},{9,1},{17,25},{25,17},{2,10},{10... | collective-permute-start | bytes 7077896 | tf_op jit(solution)/shard_map/ppermute | solution.py:336
  173.8 16.9 %collective-permute-start.44 = (bf16[4,96,384]{2,1,0:T(8,128)(2,1)S(1)}, bf16[4,96,384]{2,1,0:T(8,128)(2,1)S(1)}, u32[]{:S(2)}, u32[]{:S(2)}) collective-permute-start(bf16[4,96,384]{2,1,0:T(8,128)(2,1)S(1)} %dynamic-slice_bitcast_fusion.18), channel_id=1, source_target_pairs={{0,16},{8,24},{16,0},{24,8},{1,17},{9,25},{17,1},{25,9},{2,18},{10... | collective-permute-start | bytes 884744 | tf_op jit(solution)/shard_map/ppermute | solution.py:336
  175.0 15.8 %collective-permute-start.43 = (bf16[4,96,384]{2,1,0:T(8,128)(2,1)S(1)}, bf16[4,96,384]{2,1,0:T(8,128)(2,1)S(1)}, u32[]{:S(2)}, u32[]{:S(2)}) collective-permute-start(bf16[4,96,384]{2,1,0:T(8,128)(2,1)S(1)} %dynamic-slice_bitcast_fusion.19), channel_id=1, source_target_pairs={{0,1},{1,0},{2,3},{3,2},{4,5},{5,4},{6,7},{7,6},{8,9},{9,8},{10,11... | collective-permute-start | bytes 884744 | tf_op jit(solution)/shard_map/ppermute | solution.py:340
  175.9 17.9 %collective-permute-start.45 = (bf16[4,2,24,1536]{3,2,0,1:T(8,128)(2,1)S(1)}, bf16[4,2,24,1536]{3,2,0,1:T(8,128)(2,1)S(1)}, u32[]{:S(2)}, u32[]{:S(2)}) collective-permute-start(bf16[4,2,24,1536]{3,2,0,1:T(8,128)(2,1)S(1)} %dynamic-slice_bitcast_fusion.8), channel_id=1, source_target_pairs={{0,16},{8,24},{16,0},{24,8},{1,17},{9,25},{17,1},{25,9},{2,18},{10... | collective-permute-start | bytes 1769480 | tf_op jit(solution)/shard_map/ppermute | solution.py:336
  176.3 18.2 %collective-permute-start.46 = (bf16[2,4,24,1536]{3,2,1,0:T(8,128)(2,1)S(1)}, bf16[2,4,24,1536]{3,2,1,0:T(8,128)(2,1)S(1)}, u32[]{:S(2)}, u32[]{:S(2)}) collective-permute-start(bf16[2,4,24,1536]{3,2,1,0:T(8,128)(2,1)S(1)} %dynamic-slice_bitcast_fusion.7), channel_id=1, source_target_pairs={{0,1},{1,0},{2,3},{3,2},{4,5},{5,4},{6,7},{7,6},{8,9},{9,8},{10,11... | collective-permute-start | bytes 1769480 | tf_op jit(solution)/shard_map/ppermute | solution.py:340
  194.7 12.3 %collective-permute-start.48 = (bf16[4,24,1536]{2,1,0:T(8,128)(2,1)S(1)}, bf16[4,24,1536]{2,1,0:T(8,128)(2,1)S(1)}, u32[]{:S(2)}, u32[]{:S(2)}) collective-permute-start(bf16[4,24,1536]{2,1,0:T(8,128)(2,1)S(1)} %dynamic-slice_bitcast_fusion.16), channel_id=1, source_target_pairs={{0,16},{8,24},{16,0},{24,8},{1,17},{9,25},{17,1},{25,9},{2,18},{10... | collective-permute-start | bytes 884744 | tf_op jit(solution)/shard_map/ppermute | solution.py:336
  195.3 11.8 %collective-permute-start.47 = (bf16[4,24,1536]{2,1,0:T(8,128)(2,1)S(1)}, bf16[4,24,1536]{2,1,0:T(8,128)(2,1)S(1)}, u32[]{:S(2)}, u32[]{:S(2)}) collective-permute-start(bf16[4,24,1536]{2,1,0:T(8,128)(2,1)S(1)} %dynamic-slice_bitcast_fusion.17), channel_id=1, source_target_pairs={{0,1},{1,0},{2,3},{3,2},{4,5},{5,4},{6,7},{7,6},{8,9},{9,8},{10,11... | collective-permute-start | bytes 884744 | tf_op jit(solution)/shard_map/ppermute | solution.py:340
  196.0 12.1 %collective-permute-start.49 = (bf16[2,96,768]{2,1,0:T(8,128)(2,1)S(1)}, bf16[2,96,768]{2,1,0:T(8,128)(2,1)S(1)}, u32[]{:S(2)}, u32[]{:S(2)}) collective-permute-start(bf16[2,96,768]{2,1,0:T(8,128)(2,1)S(1)} %dynamic-slice_bitcast_fusion.15), channel_id=1, source_target_pairs={{0,2},{1,3},{2,0},{3,1},{4,6},{5,7},{6,4},{7,5},{8,10},{9,11},{10,... | collective-permute-start | bytes 884744 | tf_op jit(solution)/shard_map/ppermute | solution.py:340
  203.0 18.6 %collective-permute-start.51 = (bf16[288,768]{1,0:T(8,128)(2,1)}, bf16[288,768]{1,0:T(8,128)(2,1)}, u32[]{:S(2)}, u32[]{:S(2)}) collective-permute-start(bf16[288,768]{1,0:T(8,128)(2,1)} %get-tuple-element.245), channel_id=1, source_target_pairs={{2,0},{4,2},{5,3},{7,5},{10,8},{12,10},{13,11},{15,13},{18,16},{20... | collective-permute-start | bytes 1327112 | tf_op jit(solution)/shard_map/ppermute | solution.py:340
  204.4 19.6 %collective-permute-start.50 = (bf16[288,768]{1,0:T(8,128)(2,1)}, bf16[288,768]{1,0:T(8,128)(2,1)}, u32[]{:S(2)}, u32[]{:S(2)}) collective-permute-start(bf16[288,768]{1,0:T(8,128)(2,1)} %get-tuple-element.246), channel_id=1, source_target_pairs={{1,0},{2,1},{3,2},{4,3},{5,4},{6,5},{7,6},{9,8},{10,9},{11,10},{12... | collective-permute-start | bytes 1327112 | tf_op jit(solution)/shard_map/ppermute | solution.py:340
  224.0 8.5 %collective-permute-start.52 = (bf16[2,192,3200]{2,1,0:T(8,128)(2,1)}, bf16[2,192,3200]{2,1,0:T(8,128)(2,1)}, u32[]{:S(2)}, u32[]{:S(2)}) collective-permute-start(bf16[2,192,3200]{2,1,0:T(8,128)(2,1)} %pad_maximum_fusion), channel_id=1, source_target_pairs={{0,8},{8,0},{16,24},{24,16},{1,9},{9,1},{17,25},{25,17},{2,10},{10... | collective-permute-start | bytes 7372808 | tf_op jit(solution)/shard_map/ppermute | solution.py:336
  228.9 25.9 %collective-permute-start.57 = (bf16[96,768]{1,0:T(8,128)(2,1)S(1)}, bf16[96,768]{1,0:T(8,128)(2,1)S(1)}, u32[]{:S(2)}, u32[]{:S(2)}) collective-permute-start(bf16[96,768]{1,0:T(8,128)(2,1)S(1)} %slice.178), channel_id=1, source_target_pairs={{5,2},{13,10},{21,18},{29,26}} | collective-permute-start | bytes 442376 | tf_op jit(solution)/shard_map/ppermute | solution.py:340
  235.4 9.2 %collective-permute-start.56 = (bf16[96,768]{1,0:T(8,128)(2,1)S(1)}, bf16[96,768]{1,0:T(8,128)(2,1)S(1)}, u32[]{:S(2)}, u32[]{:S(2)}) collective-permute-start(bf16[96,768]{1,0:T(8,128)(2,1)S(1)} %dynamic-slice_bitcast_fusion.22), channel_id=1, source_target_pairs={{0,4},{1,5},{2,6},{3,7},{4,0},{5,1},{6,2},{7,3},{8,12},{9,13},{10,... | collective-permute-start | bytes 442376 | tf_op jit(solution)/shard_map/ppermute | solution.py:340
  236.7 11.5 %collective-permute-start.55 = (bf16[2,24,3072]{2,1,0:T(8,128)(2,1)S(1)}, bf16[2,24,3072]{2,1,0:T(8,128)(2,1)S(1)}, u32[]{:S(2)}, u32[]{:S(2)}) collective-permute-start(bf16[2,24,3072]{2,1,0:T(8,128)(2,1)S(1)} %dynamic-slice_bitcast_fusion.14), channel_id=1, source_target_pairs={{0,2},{1,3},{2,0},{3,1},{4,6},{5,7},{6,4},{7,5},{8,10},{9,11},{10,... | collective-permute-start | bytes 884744 | tf_op jit(solution)/shard_map/ppermute | solution.py:340
  238.7 14.0 %collective-permute-start.53 = (bf16[4,2,24,1536]{3,2,0,1:T(8,128)(2,1)S(1)}, bf16[4,2,24,1536]{3,2,0,1:T(8,128)(2,1)S(1)}, u32[]{:S(2)}, u32[]{:S(2)}) collective-permute-start(bf16[4,2,24,1536]{3,2,0,1:T(8,128)(2,1)S(1)} %bitcast.290), channel_id=1, source_target_pairs={{0,16},{8,24},{16,0},{24,8},{1,17},{9,25},{17,1},{25,9},{2,18},{10... | collective-permute-start | bytes 1769480 | tf_op jit(solution)/shard_map/ppermute | solution.py:336
  239.9 14.7 %collective-permute-start.54 = (bf16[2,4,24,1664]{3,2,1,0:T(8,128)(2,1)S(1)}, bf16[2,4,24,1664]{3,2,1,0:T(8,128)(2,1)S(1)}, u32[]{:S(2)}, u32[]{:S(2)}) collective-permute-start(bf16[2,4,24,1664]{3,2,1,0:T(8,128)(2,1)S(1)} %dynamic-slice_bitcast_fusion.2), channel_id=1, source_target_pairs={{0,1},{1,0},{2,3},{3,2},{4,5},{5,4},{6,7},{7,6},{8,9},{9,8},{10,11... | collective-permute-start | bytes 1916936 | tf_op jit(solution)/shard_map/ppermute | solution.py:340
  256.7 9.1 %collective-permute-start.65 = (bf16[24,3072]{1,0:T(8,128)(2,1)S(1)}, bf16[24,3072]{1,0:T(8,128)(2,1)S(1)}, u32[]{:S(2)}, u32[]{:S(2)}) collective-permute-start(bf16[24,3072]{1,0:T(8,128)(2,1)S(1)} %dynamic-slice_bitcast_fusion.21), channel_id=1, source_target_pairs={{0,4},{1,5},{2,6},{3,7},{4,0},{5,1},{6,2},{7,3},{8,12},{9,13},{10,... | collective-permute-start | bytes 442376 | tf_op jit(solution)/shard_map/ppermute | solution.py:340
  257.5 6.2 %collective-permute-start.58 = (bf16[4,24,1536]{2,1,0:T(8,128)(2,1)S(1)}, bf16[4,24,1536]{2,1,0:T(8,128)(2,1)S(1)}, u32[]{:S(2)}, u32[]{:S(2)}) collective-permute-start(bf16[4,24,1536]{2,1,0:T(8,128)(2,1)S(1)} %dynamic-slice_bitcast_fusion.13), channel_id=1, source_target_pairs={{0,1},{1,0},{2,3},{3,2},{4,5},{5,4},{6,7},{7,6},{8,9},{9,8},{10,11... | collective-permute-start | bytes 884744 | tf_op jit(solution)/shard_map/ppermute | solution.py:340
  258.2 6.7 %collective-permute-start.59 = (bf16[4,24,1664]{2,1,0:T(8,128)(2,1)S(1)}, bf16[4,24,1664]{2,1,0:T(8,128)(2,1)S(1)}, u32[]{:S(2)}, u32[]{:S(2)}) collective-permute-start(bf16[4,24,1664]{2,1,0:T(8,128)(2,1)S(1)} %dynamic-slice_bitcast_fusion.11), channel_id=1, source_target_pairs={{0,16},{8,24},{16,0},{24,8},{1,17},{9,25},{17,1},{25,9},{2,18},{10... | collective-permute-start | bytes 958472 | tf_op jit(solution)/shard_map/ppermute | solution.py:336
  265.0 5.8 %collective-permute-start.60 = (bf16[2,24,3200]{2,1,0:T(8,128)(2,1)S(1)}, bf16[2,24,3200]{2,1,0:T(8,128)(2,1)S(1)}, u32[]{:S(2)}, u32[]{:S(2)}) collective-permute-start(bf16[2,24,3200]{2,1,0:T(8,128)(2,1)S(1)} %dynamic-slice_bitcast_fusion.12), channel_id=1, source_target_pairs={{0,2},{1,3},{2,0},{3,1},{4,6},{5,7},{6,4},{7,5},{8,10},{9,11},{10,... | collective-permute-start | bytes 921608 | tf_op jit(solution)/shard_map/ppermute | solution.py:340
  270.9 8.4 %collective-permute-start.64 = (bf16[24,3200]{1,0:T(8,128)(2,1)S(1)}, bf16[24,3200]{1,0:T(8,128)(2,1)S(1)}, u32[]{:S(2)}, u32[]{:S(2)}) collective-permute-start(bf16[24,3200]{1,0:T(8,128)(2,1)S(1)} %dynamic-slice_bitcast_fusion.20), channel_id=1, source_target_pairs={{0,4},{1,5},{2,6},{3,7},{4,0},{5,1},{6,2},{7,3},{8,12},{9,13},{10,... | collective-permute-start | bytes 460808 | tf_op jit(solution)/shard_map/ppermute | solution.py:340
  272.1 28.0 %collective-permute-start.62 = (bf16[192,768]{1,0:T(8,128)(2,1)S(1)}, bf16[192,768]{1,0:T(8,128)(2,1)S(1)}, u32[]{:S(2)}, u32[]{:S(2)}) collective-permute-start(bf16[192,768]{1,0:T(8,128)(2,1)S(1)} %bitcast.296), channel_id=1, source_target_pairs={{0,1},{1,4},{2,7},{3,2},{4,5},{5,0},{6,3},{7,6},{8,9},{9,12},{10,1... | collective-permute-start | bytes 884744 | tf_op jit(solution)/shard_map/ppermute | solution.py:340
  273.8 26.4 %collective-permute-start.63 = (bf16[192,768]{1,0:T(8,128)(2,1)S(1)}, bf16[192,768]{1,0:T(8,128)(2,1)S(1)}, u32[]{:S(2)}, u32[]{:S(2)}) collective-permute-start(bf16[192,768]{1,0:T(8,128)(2,1)S(1)} %bitcast.295), channel_id=1, source_target_pairs={{0,2},{1,5},{2,0},{3,3},{4,6},{5,1},{6,4},{7,7},{8,10},{9,13},{10,... | collective-permute-start | bytes 884744 | tf_op jit(solution)/shard_map/ppermute | solution.py:340
  277.4 22.7 %collective-permute-start.61 = (bf16[192,768]{1,0:T(8,128)(2,1)S(1)}, bf16[192,768]{1,0:T(8,128)(2,1)S(1)}, u32[]{:S(2)}, u32[]{:S(2)}) collective-permute-start(bf16[192,768]{1,0:T(8,128)(2,1)S(1)} %bitcast.297), channel_id=1, source_target_pairs={{0,0},{1,3},{2,6},{3,1},{4,4},{5,7},{6,2},{7,5},{8,8},{9,11},{10,1... | collective-permute-start | bytes 884744 | tf_op jit(solution)/shard_map/ppermute | solution.py:340
  (77 other events, 467.4 us)
